TPU v7x, 256 devices: a whole 4x4x8 slice. The times are simulated.
256 devices in a mesh: tm: 64 (over x, z, core), region: 4 (over y).
Axes of the slice: x: 4, y: 4, z: 8, core: 2. Of those that a mesh axis runs over, the one named last changes fastest.
Arguments:
- solution: float32 [8192, 4096], P('tm', 'region'), may hold values from -6 to 6
- residual: float32 [8192, 4096], P('tm', 'region'), may hold values from -50 to 50
- direction: float32 [8192, 4096], P('tm', 'region'), may hold values from -50 to 50
- decay: float32 [8192, 4096], P('tm', 'region'), may hold values from 0 to 1, as said below
- spatial: bfloat16 [4096, 4096], P('region'), may hold values from -1 to 2, as said below
- tiles: bfloat16 [64, 4, 8, 128, 512], P('tm', 'region'), may hold values from -0.1875 to 0.1875
- tile_block: int32 [64, 4, 8], P('tm', 'region'), may hold values from 0 to 7
- tile_time: int32 [64, 4, 8], P('tm', 'region'), may hold values from 0 to 383
- tile_cell: int32 [64, 4, 8], P('tm', 'region'), may hold values from 0 to 1
- tile_count: int32 [64, 4], P('tm', 'region'), may hold values from 1 to 8, as said below
- noise_inv: float32 [512, 128], P('tm'), may hold values from 0.25 to 2
Outputs:
- solution_new: float32 [8192, 4096], P('tm', 'region')
- residual_new: float32 [8192, 4096], P('tm', 'region')
- direction_new: float32 [8192, 4096], P('tm', 'region')
Inputs may be any that keep to these rules, and one draw needn't show every extreme that they name: Slots 0 to tile_count - 1 of a window and region hold tiles, the rest are padding; some window and region has 8. `decay`: strictly between 0 and 1. `spatial`: symmetric.
All inputs are finite; a program needn't handle non-finite values.
Results may differ from a plain program's by a relative error of at most 0.0028.
Values may be sent and summed in bfloat16 or wider, within the bound.
A program may use at most 64 MiB of HBM per device.

v0:
```python
import jax
import jax.numpy as jnp
from jax import lax
from jax.sharding import PartitionSpec as P

FB = 512
BACK = 2


def carried_in(part, axis, combine, identity, reverse):
    count = lax.axis_size(axis)
    place = lax.axis_index(axis)
    ahead = count - 1 - place if reverse else place
    gathered = jax.tree.map(lambda a: lax.all_gather(a, axis), part)
    state = jax.tree.map(lambda a, e: jnp.zeros_like(a) + jnp.asarray(e, a.dtype), part, identity)

    def one(hop, state):
        source = count - 1 - hop if reverse else hop
        return combine(
            state, jax.tree.map(lambda a: lax.dynamic_index_in_dim(a, source, 0, False), gathered)
        )

    return lax.fori_loop(0, ahead, one, state)


def shifted(block, axis, distance):
    devices = range(lax.axis_size(axis))
    route = [(i - distance, i) for i in devices if i - distance in devices]
    return lax.ppermute(block, axis, route)


def compose(earlier, later):
    return (earlier[0] * later[0], later[0] * earlier[1] + later[1])


def body(
    solution,
    residual,
    direction,
    decay,
    spatial,
    tiles,
    tile_block,
    tile_time,
    tile_cell,
    tile_count,
    noise_inv,
):
    precise = lax.Precision.HIGHEST
    window_len, row_width = direction.shape
    span_len = (BACK + 1) * window_len
    cell_blocks = row_width // FB
    footprint = tiles[0, 0]
    blocks = tile_block[0, 0]
    tile_times = tile_time[0, 0]
    tile_cells = tile_cell[0, 0]
    live_count = tile_count[0, 0]
    capacity = footprint.shape[0]
    block_count = noise_inv.shape[0]
    norm_old = lax.psum(jnp.sum(residual * residual), ("tm", "region"))
    gain_in = jnp.sqrt(1.0 - decay * decay)
    dir_half = direction.astype(jnp.bfloat16)
    mixed_cells = lax.dot_general(
        lax.all_gather(dir_half, "region", axis=1, tiled=True),
        spatial,
        (((1,), (1,)), ((), ())),
        preferred_element_type=jnp.float32,
    )
    factors, offsets = lax.associative_scan(compose, (decay, gain_in * mixed_cells), axis=0)
    identity_pair = (jnp.ones((row_width,), jnp.float32), jnp.zeros((row_width,), jnp.float32))
    entered = carried_in((factors[-1], offsets[-1]), "tm", compose, identity_pair, False)
    filtered = offsets + factors * entered[1][None, :]
    coarse = filtered.astype(jnp.bfloat16)
    pieces = [coarse]
    for hop_count in range(1, BACK + 1):
        pieces.insert(0, shifted(coarse, "tm", hop_count))
    window = jnp.concatenate(pieces, axis=0).reshape(span_len, cell_blocks, FB)
    block_ids = jnp.arange(block_count, dtype=jnp.int32)
    place_ids = jnp.arange(span_len * cell_blocks, dtype=jnp.int32)
    is_live = jnp.arange(capacity, dtype=jnp.int32) < live_count
    chosen = window[tile_times, tile_cells]
    partial_obs = jnp.einsum("jkc,jc->jk", footprint, chosen, preferred_element_type=jnp.float32)
    block_hot = ((blocks[None, :] == block_ids[:, None]) & is_live[None, :]).astype(jnp.float32)
    summed_obs = jnp.dot(
        block_hot, partial_obs, precision=precise, preferred_element_type=jnp.float32
    )
    observed = lax.psum(summed_obs, "region")
    weighted = (observed * noise_inv).astype(jnp.bfloat16)
    picked = weighted[blocks]
    partial_back = jnp.einsum("jkc,jk->jc", footprint, picked, preferred_element_type=jnp.float32)
    epoch_index = tile_times * cell_blocks + tile_cells
    place_hot = ((epoch_index[None, :] == place_ids[:, None]) & is_live[None, :]).astype(
        jnp.float32
    )
    spread_time = jnp.dot(
        place_hot, partial_back, precision=precise, preferred_element_type=jnp.float32
    ).reshape(span_len, row_width)
    segments = [
        spread_time[seg_idx * window_len : (seg_idx + 1) * window_len]
        for seg_idx in range(BACK + 1)
    ]
    adjoint = segments[BACK]
    for hop_count in range(1, BACK + 1):
        adjoint = adjoint + shifted(segments[BACK - hop_count], "tm", -hop_count)
    back_factors, back_offsets = lax.associative_scan(
        compose, (decay, decay * adjoint), reverse=True, axis=0
    )
    leaving = carried_in((back_factors[0], back_offsets[0]), "tm", compose, identity_pair, True)
    incoming = leaving[1]
    later_state = jnp.concatenate(
        [back_offsets[1:] + back_factors[1:] * incoming[None, :], incoming[None, :]], axis=0
    )
    held_sum = adjoint + later_state
    pulled = (gain_in * held_sum).astype(jnp.bfloat16)
    contribution = jnp.dot(pulled, spatial, preferred_element_type=jnp.float32)
    spread = lax.psum_scatter(contribution, "region", scatter_dimension=1, tiled=True)
    op_image = direction + spread
    curvature = lax.psum(jnp.sum(direction * op_image), ("tm", "region"))
    step_len = norm_old / curvature
    residual_new = residual - step_len * op_image
    norm_new = lax.psum(jnp.sum(residual_new * residual_new), ("tm", "region"))
    solution_new = solution + step_len * direction
    direction_new = residual_new + norm_new / norm_old * direction
    return (solution_new, residual_new, direction_new)


def solution(mesh):
    return jax.shard_map(
        body,
        mesh=mesh,
        in_specs=(
            P("tm", "region"),
            P("tm", "region"),
            P("tm", "region"),
            P("tm", "region"),
            P("region", None),
            P("tm", "region", None, None, None),
            P("tm", "region", None),
            P("tm", "region", None),
            P("tm", "region", None),
            P("tm", "region"),
            P("tm", None),
        ),
        out_specs=(P("tm", "region"), P("tm", "region"), P("tm", "region")),
        check_vma=False,
    )
```

profile of v0, /device:TPU:1, one launch (start us, length us, event | category | flops | bytes accessed | tf_op | source)
XLA Modules:
  0.0 647.8 jit_solution(11329008263642643065)
XLA Ops:
  14.1 25.8 %all-gather.6.cloned.1.call-done = bf16[128,4096]{1,0:T(8,128)(2,1)} async-done(((bf16[128,1024]{1,0:T(8,128)(2,1)}), bf16[128,4096]{1,0:T(8,128)(2,1)}) %all-gather.6.cloned.1.call-update) | async-done | bytes 1048592 | tf_op jit(solution)/shard_map/all_gather | solution.py:64
  39.9 6.6 %convolution_multiply_fusion = f32[128,1024]{1,0:T(8,128)S(1)} fusion(bf16[128,4096]{1,0:T(8,128)(2,1)} %all-gather.6.cloned.1.call-done, bf16[1024,4096]{1,0:T(8,128)(2,1)} %param.19, f32[128,1024]{1,0:T(8,128)S(1)} %copy-done.1), kind=kOutput, calls=%fused_computation.8 | convolution fusion | flops 1074135040 | bytes 10485760 | tf_op jit(solution)/shard_map/dot_general | solution.py:63
  55.0 2.6 pad.199
  61.1 46.5 %all-gather = f32[64,1,1024]{2,1,0:T(1,128)S(1)} all-gather(f32[1,1,1024]{2,1,0:T(1,128)S(1)} %add_bitcast_fusion.1), channel_id=1, replica_groups=mesh['tm'=64,'region'=4] {'tm'}, dimensions={0}, use_global_device_ids=true | all-gather | bytes 266240 | tf_op jit(solution)/shard_map/all_gather | solution.py:14
  108.3 2.6 pad.185
  112.6 2.6 pad.184
  116.0 42.8 %all-gather.1 = f32[64,1,1024]{2,1,0:T(1,128)S(1)} all-gather(f32[1,1,1024]{2,1,0:T(1,128)S(1)} %add_bitcast_fusion), channel_id=1, replica_groups=mesh['tm'=64,'region'=4] {'tm'}, dimensions={0}, use_global_device_ids=true | all-gather | bytes 266240 | tf_op jit(solution)/shard_map/all_gather | solution.py:14
  161.8 3.4 collective-permute-start.1
  165.2 4.1 collective-permute-start
  169.4 5.5 collective-permute-done
  178.2 7.5 %psum.29 = f32[8,128]{1,0:T(8,128)S(1)} all-reduce(f32[8,128]{1,0:T(8,128)S(1)} %fusion.37), channel_id=1, replica_groups=mesh['tm'=64,'region'=4] {'region'}, use_global_device_ids=true, to_apply=%region_4.5 | all-reduce | flops 1024 | bytes 8192 | tf_op jit(solution)/shard_map/psum | solution.py:87
  191.6 4.1 collective-permute-start.2
  204.9 7.7 %collective-permute-done.2 = f32[128,1024]{1,0:T(8,128)} collective-permute-done((f32[128,1024]{1,0:T(8,128)}, f32[128,1024]{1,0:T(8,128)}, u32[]{:S(2)}, u32[]{:S(2)}) %collective-permute-start.2) | collective-permute-done | bytes 524320 | tf_op jit(solution)/shard_map/ppermute | solution.py:29
  215.4 4.3 slice.537
  219.7 4.3 slice.539
  252.2 4.8 slice.603
  259.4 88.4 %all-gather.3 = f32[64,1,1024]{2,1,0:T(1,128)S(1)} all-gather(f32[1,1,1024]{2,1,0:T(1,128)S(1)} %get-tuple-element.230), channel_id=1, replica_groups=mesh['tm'=64,'region'=4] {'tm'}, dimensions={0}, use_global_device_ids=true | all-gather | bytes 266240 | tf_op jit(solution)/shard_map/all_gather | solution.py:14
  353.1 4.8 slice.588
  357.9 43.8 %all-gather.2 = f32[64,1,1024]{2,1,0:T(1,128)S(1)} all-gather(f32[1,1,1024]{2,1,0:T(1,128)S(1)} %get-tuple-element.231), channel_id=1, replica_groups=mesh['tm'=64,'region'=4] {'tm'}, dimensions={0}, use_global_device_ids=true | all-gather | bytes 266240 | tf_op jit(solution)/shard_map/all_gather | solution.py:14
  401.8 49.5 %while.27 = (s32[]{:T(128)}, f32[1024]{0:T(1024)S(1)}, s32[]{:T(128)}, f32[64,1024]{1,0:T(8,128)S(1)}, f32[64,1024]{1,0:T(8,128)}, /*index=5*/s32[]{:T(128)}, s32[]{:T(128)}, s32[]{:T(128)}, s32[]{:T(128)}) while((s32[]{:T(128)}, f32[1024]{0:T(1024)S(1)}, s32[]{:T(128)}, f32[64,1024]{1,0:T(8,128)S(1)}, f32[64,1024]{1,0:T(8,128)}, ...), condition=%wide.region_6.7_spmd, body=%wide.region_5.6_spmd.sunk | while | flops 2054 | bytes 32919 | solution.py:23
  452.6 6.3 fusion.9
  460.6 22.9 %reduce-scatter.2.cloned.1.call-done = f32[128,1024]{1,0:T(8,128)} async-done(((f32[128,4096]{1,0:T(8,128)}), f32[128,1024]{1,0:T(8,128)}) %reduce-scatter.2.cloned.1.call-update) | async-done | bytes 524304 | tf_op jit(solution)/shard_map/reduce_scatter | solution.py:116
  485.3 76.0 %all-reduce.56 = (f32[]{:T(128)}, f32[]{:T(128)}) all-reduce(f32[]{:T(128)} %multiply_reduce_fusion.2, f32[]{:T(128)} %get-tuple-element.157), channel_id=1, replica_groups=mesh['tm'=64,'region'=4] {'tm','region'}, use_global_device_ids=true, to_apply=%region_1.0 | all-reduce | flops 2 | bytes 16 | tf_op jit(solution)/shard_map/psum | solution.py:60
  563.4 74.1 %psum.31 = f32[]{:T(128)} all-reduce(f32[]{:T(128)} %get-tuple-element.155), channel_id=1, replica_groups=mesh['tm'=64,'region'=4] {'tm','region'}, use_global_device_ids=true, to_apply=%region_11.12 | all-reduce | flops 1 | bytes 8 | tf_op jit(solution)/shard_map/psum | solution.py:121
  (418 shorter events, 137.4 us)
Async XLA Ops:
  7.2 170.6 %copy-start = (bf16[1,1,8,128,512]{4,3,2,1,0:T(8,128)(2,1)S(1)}, bf16[1,1,8,128,512]{4,3,2,1,0:T(8,128)(2,1)}, u32[]{:S(2)}) copy-start(bf16[1,1,8,128,512]{4,3,2,1,0:T(8,128)(2,1)} %param.20) | copy-start | bytes 3145732
  7.2 4.2 copy-start.1
  7.2 5.7 copy-start.13
  7.2 6.3 copy-start.15
  7.2 6.3 copy-start.17
  7.2 32.7 %all-gather.6.cloned.1.call-start = ((), (), s32[]{:S(2)}) async-start(), calls=%async_computation.1 | async-start | bytes 1310720 | tf_op jit(solution)/shard_map/all_gather | solution.py:64
  9.2 474.3 %reduce-scatter.2.cloned.1.call-start = ((), (), s32[]{:S(2)}) async-start(), calls=%async_computation.2 | async-start | bytes 2621440 | tf_op jit(solution)/shard_map/reduce_scatter | solution.py:116
  46.6 3.8 copy-start.3
  54.2 6.0 copy-start.11
  58.3 52.6 %slice-start = ((f32[128,1024]{1,0:T(8,128)}), f32[1,1024]{1,0:T(1,128)S(1)}, s32[]{:S(2)}) async-start(f32[128,1024]{1,0:T(8,128)} %copy-done.3), calls=%async_computation.3 | async-start | bytes 8192 | tf_op jit(solution)/shard_map/slice | solution.py:69
  60.3 100.1 %copy-start.4 = (f32[128,1024]{1,0:T(8,128)S(1)}, f32[128,1024]{1,0:T(8,128)}, u32[]{:S(2)}) copy-start(f32[128,1024]{1,0:T(8,128)} %pad.199) | copy-start | bytes 1572868
  112.6 56.7 %copy-start.16 = (s32[1,1,8]{2,1,0:T(1,128)S(1)}, s32[1,1,8]{2,1,0:T(1,128)}, u32[]{:S(2)}) copy-start(s32[1,1,8]{2,1,0:T(1,128)} %param.23) | copy-start | bytes 100
  112.6 56.7 %copy-start.18 = (s32[1,1,8]{2,1,0:T(1,128)S(1)}, s32[1,1,8]{2,1,0:T(1,128)}, u32[]{:S(2)}) copy-start(s32[1,1,8]{2,1,0:T(1,128)} %param.22) | copy-start | bytes 100
  161.8 7.6 %collective-permute-start.1 = (bf16[128,1024]{1,0:T(8,128)(2,1)S(1)}, bf16[128,1024]{1,0:T(8,128)(2,1)S(1)}, u32[]{:S(2)}, u32[]{:S(2)}) collective-permute-start(bf16[128,1024]{1,0:T(8,128)(2,1)S(1)} %add_convert_fusion), channel_id=1, source_target_pairs={{0,4},{4,8},{8,12},{12,16},{16,20},{20,24},{24,28},{28,32},{32,36}... | collective-permute-start | bytes 786440 | tf_op jit(solution)/shard_map/ppermute | solution.py:29
  165.2 9.8 %collective-permute-start = (bf16[128,1024]{1,0:T(8,128)(2,1)S(1)}, bf16[128,1024]{1,0:T(8,128)(2,1)S(1)}, u32[]{:S(2)}, u32[]{:S(2)}) collective-permute-start(bf16[128,1024]{1,0:T(8,128)(2,1)S(1)} %add_convert_fusion), channel_id=1, source_target_pairs={{0,8},{4,12},{8,16},{12,20},{16,24},{20,28},{24,32},{28,36},{32,40... | collective-permute-start | bytes 786440 | tf_op jit(solution)/shard_map/ppermute | solution.py:29
  169.4 8.7 %copy-start.14 = (s32[1,1,8]{2,1,0:T(1,128)S(1)}, s32[1,1,8]{2,1,0:T(1,128)}, u32[]{:S(2)}) copy-start(s32[1,1,8]{2,1,0:T(1,128)} %param.21) | copy-start | bytes 100
  169.4 16.3 %copy-start.12 = (f32[8,128]{1,0:T(8,128)S(1)}, f32[8,128]{1,0:T(8,128)}, u32[]{:S(2)}) copy-start(f32[8,128]{1,0:T(8,128)} %param.25) | copy-start | bytes 12292
  190.3 14.6 %collective-permute-start.3 = (f32[128,1024]{1,0:T(8,128)}, f32[128,1024]{1,0:T(8,128)S(1)}, u32[]{:S(2)}, u32[]{:S(2)}) collective-permute-start(f32[128,1024]{1,0:T(8,128)} %slice.531), channel_id=1, source_target_pairs={{8,0},{12,4},{16,8},{20,12},{24,16},{28,20},{32,24},{36,28},{40,32... | collective-permute-start | bytes 1572872 | tf_op jit(solution)/shard_map/ppermute | solution.py:29
  191.6 21.0 %collective-permute-start.2 = (f32[128,1024]{1,0:T(8,128)}, f32[128,1024]{1,0:T(8,128)}, u32[]{:S(2)}, u32[]{:S(2)}) collective-permute-start(f32[128,1024]{1,0:T(8,128)} %slice.529), channel_id=1, source_target_pairs={{4,0},{8,4},{12,8},{16,12},{20,16},{24,20},{28,24},{32,28},{36,32}... | collective-permute-start | bytes 1572872 | tf_op jit(solution)/shard_map/ppermute | solution.py:29
  230.5 3.7 copy-start.10
  233.9 2.6 copy-start.8
  233.9 2.6 copy-start.9
  458.9 24.6 %copy-start.2 = (f32[128,1024]{1,0:T(8,128)S(1)}, f32[128,1024]{1,0:T(8,128)}, u32[]{:S(2)}) copy-start(f32[128,1024]{1,0:T(8,128)} %param.17) | copy-start | bytes 1572868
  563.4 77.6 %copy-start.5 = (f32[128,1024]{1,0:T(8,128)}, f32[128,1024]{1,0:T(8,128)S(1)}, u32[]{:S(2)}) copy-start(f32[128,1024]{1,0:T(8,128)S(1)} %get-tuple-element.156) | copy-start | bytes 1572868
  (2 other events, 1.9 us)
Sparse Core Ops, SparseCore 0:
  10.4 29.4 all-gather.5
  459.0 24.4 reduce-scatter.1
where the time goes:
time: 655 us; the launch traced here: 648 us
  blocking collectives  379 us (58%)
  local copies, waits for them, and re-layouts  123 us (19%)
  waiting for transfers between devices  62 us (9%)
  other arithmetic  36.4 us (6%)
  between operations  18.7 us (3%)
  matrix products  14.4 us (2%)
  starting transfers between devices  13 us (2%)
    all_gather x4, blocking collectives, carried_in(): gathered = jax.tree.map(lambda a: lax.all_gather(a, axis), part)  221 us
    psum x1, blocking collectives, body(): norm_old = lax.psum(jnp.sum(residual * residual), ('tm', 'region'))  76 us
    psum x1, blocking collectives, body(): norm_new = lax.psum(jnp.sum(residual_new * residual_new), ('tm', 'region'))  74.1 us
    dynamic_slice x63, local copies, waits for them, and re-layouts, one(): lax.dynamic_index_in_dim(a, source, 0, False)  48.6 us
    slice x48, local copies, waits for them, and re-layouts, body(): lax.associative_scan(compose, (decay, decay * adjoint), reverse=True, axi...  25.9 us
    all_gather x1, waiting for transfers between devices, body(): lax.all_gather(dir_half, 'region', axis=1, tiled=True)  25.8 us
    reduce_scatter x1, waiting for transfers between devices, body(): lax.psum_scatter(contribution, 'region', scatter_dimension=1, tiled=True)  22.9 us
    ppermute x4, waiting for transfers between devices, shifted(): return lax.ppermute(block, axis, route)  13.4 us
  transfers between devices with their start and end apart: 6, of which 5 were waited for; matrix products, arithmetic and copies ran while one was open for 2% of the time, Pallas kernels for 0%

commit v1 on v0

v1 whole, which is shorter than its diff:
```python
import jax
import jax.numpy as jnp
from jax import lax
from jax.experimental import pallas as pl
from jax.experimental.pallas import tpu as pltpu
from jax.sharding import PartitionSpec as P

MESH = pl.DeviceIdType.MESH
TW = 128
RC = 1024
FB = 512
SLOTS = 8
LINE = 16
LINES = 4
REGIONS = 4
WINDOWS = LINE * LINES
CH = 8
ST = TW // CH
PIECES = RC // 128
DEAD = -8192
F32 = jnp.float32
BF16 = jnp.bfloat16
NT = (((1,), (1,)), ((), ()))
TN = (((0,), (0,)), ((), ()))


def kernel(
    dir_h, res_h, dec_h, spa_h, tiles_h, tblock, ttime, tcell, tcount, noise,
    img, ab,
    dirv, resv, decv, spa, tiles, xa, xb, dp, gp, fp, rp, mx, hx, fstep, bstep, ends,
    abuf, gabuf, bbuf, tbuf, cbuf, ubuf, tabs, chs, bks, obs, red1, red2, sel,
    lsem, gas, gar, gbs, gbr, as_, ar, a2s, a2r, bs, br, b2s, b2r, cs, cr, c2s, c2r,
    ts, tr, hs, hr, ks, kr, os_, or_, r1s, r1r, r2s, r2r,
):
    tm = lax.axis_index("tm")
    r = lax.axis_index("region")
    gx = tm // LINE
    gi = lax.rem(tm, LINE)

    loads = [pltpu.make_async_copy(dir_h, dirv, lsem.at[0])]
    for k in range(REGIONS):
        src = lax.rem(r + REGIONS - k, REGIONS)
        cols = pl.ds(pl.multiple_of(src * RC, RC), RC)
        loads.append(pltpu.make_async_copy(spa_h.at[:, cols], spa.at[k], lsem.at[1 + k]))
    loads.append(pltpu.make_async_copy(tiles_h.at[0, 0], tiles, lsem.at[5]))
    loads.append(pltpu.make_async_copy(res_h, resv, lsem.at[6]))
    for n in range(PIECES):
        loads.append(pltpu.make_async_copy(dec_h.at[:, 128 * n : 128 * (n + 1)], decv.at[n], lsem.at[7 + n]))
    load_dir, load_spa, load_tiles, load_res, load_dec = loads[0], loads[1:5], loads[5], loads[6], loads[7:]
    for c in loads:
        c.start()

    line_peers = [(gx * LINE + lax.rem(gi + k, LINE), r) for k in range(1, LINE)]
    cross_peers = [(lax.rem(gx + k, LINES) * LINE + gi, r) for k in range(1, LINES)]
    region_peers = [(tm, lax.rem(r + k, REGIONS)) for k in range(1, REGIONS)]
    plane_peers = [
        (lax.rem(gx + kx, LINES) * LINE + gi, lax.rem(r + ky, REGIONS))
        for kx in range(LINES)
        for ky in range(REGIONS)
        if kx or ky
    ]
    later = [(lax.rem(tm + d, WINDOWS), r) for d in (1, 2)]
    sooner = [(lax.rem(tm + WINDOWS - d, WINDOWS), r) for d in (1, 2)]

    barrier = pltpu.get_barrier_semaphore()
    everyone = line_peers + plane_peers + later + sooner
    for peer in everyone:
        pl.semaphore_signal(barrier, inc=1, device_id=peer, device_id_type=MESH)

    def send(src, dst, ss, rs, peer):
        c = pltpu.make_async_remote_copy(
            src_ref=src, dst_ref=dst, send_sem=ss, recv_sem=rs, device_id=peer, device_id_type=MESH
        )
        c.start()
        return c

    def to_all(ref, ss, rs, peers):
        return [send(ref, ref, ss.at[k], rs.at[k], peer) for k, peer in enumerate(peers)]

    def wait_all(copies):
        for c in copies:
            c.wait()

    sub8 = lax.broadcasted_iota(jnp.int32, (CH, RC), 0)
    sub = lax.broadcasted_iota(jnp.int32, (8, 128), 0)

    load_dir.wait()
    row = lax.broadcasted_iota(jnp.int32, (TW, TW), 0)
    col = lax.broadcasted_iota(jnp.int32, (TW, TW), 1)
    moved = jnp.where(lax.rem(row, CH) * ST + row // CH == col, 1.0, 0.0).astype(BF16)
    xa[0] = jnp.dot(moved, dirv[...].astype(BF16), preferred_element_type=F32).astype(BF16)

    pl.semaphore_wait(barrier, len(everyone))

    low, high = pl.ds(0, TW // 2), pl.ds(TW // 2, TW // 2)
    right = (tm, lax.rem(r + 1, REGIONS))
    left = (tm, lax.rem(r + REGIONS - 1, REGIONS))

    def gather_start(x, ss, rs):
        return [
            send(x.at[0, low], x.at[1, low], ss.at[0], rs.at[0], right),
            send(x.at[0, high], x.at[3, high], ss.at[1], rs.at[1], left),
            send(x.at[0, high], x.at[1, high], ss.at[2], rs.at[2], right),
            send(x.at[0, low], x.at[3, low], ss.at[3], rs.at[3], left),
        ]

    def gather_pass(x, ss, rs, copies):
        copies[0].wait_recv()
        copies.append(send(x.at[1, low], x.at[2, low], ss.at[4], rs.at[4], right))
        copies[1].wait_recv()
        copies.append(send(x.at[3, high], x.at[2, high], ss.at[5], rs.at[5], left))

    def multiply(x, k, first):
        def tile(n, _):
            cols = pl.ds(pl.multiple_of(n * 256, 256), 256)
            part = lax.dot_general(x[k], spa[k, cols, :], NT, preferred_element_type=F32)
            if first:
                mx[:, cols] = part
            else:
                mx[:, cols] += part
            return 0

        lax.fori_loop(0, RC // 256, tile, 0)

    def gather_multiply(x, ss, rs, copies, between):
        between()
        gather_pass(x, ss, rs, copies)
        multiply(x, 0, True)
        copies[2].wait_recv()
        multiply(x, 1, False)
        copies[3].wait_recv()
        multiply(x, 3, False)
        copies[4].wait_recv()
        copies[5].wait_recv()
        multiply(x, 2, False)
        for c in copies:
            c.wait_send()

    def steps(i):
        return slice(CH * i, CH * (i + 1))

    def prepare():
        table = jnp.full((8, 128), DEAD, jnp.int32)
        for s in range(SLOTS):
            key = jnp.where(s < tcount[0, 0], ttime[0, 0, s] * 2 + tcell[0, 0, s], DEAD)
            table = jnp.where(sub == s, key, table)
        tabs[0] = table
        table_copies = [
            send(tabs.at[0], tabs.at[d], ts.at[d - 1], tr.at[d - 1], sooner[d - 1]) for d in (1, 2)
        ]
        for load in load_dec:
            load.wait()
        f = jnp.ones((CH, RC), F32)
        for i in range(ST):
            d = jnp.concatenate([decv[n, pl.ds(i, CH, stride=ST), :] for n in range(PIECES)], axis=1)
            dp[steps(i), :] = d
            gp[steps(i), :] = jnp.sqrt(1.0 - d * d)
            f = f * d
            fp[steps(i), :] = f
        total = f
        for n, k in enumerate((1, 2, 4)):
            fstep[n] = f
            f = f * jnp.where(sub8 >= k, pltpu.roll(f, k, 0), 1.0)
        ends[0] = jnp.where(sub8 >= 1, pltpu.roll(f, 1, 0), 1.0)
        abuf[gi] = f[CH - 1 : CH, :]
        factor_copies = to_all(abuf.at[gi], as_, ar, line_peers)
        b = total
        for n, k in enumerate((1, 2, 4)):
            bstep[n] = b
            b = b * jnp.where(sub8 < CH - k, pltpu.roll(b, CH - k, 0), 1.0)
        ends[1] = jnp.where(sub8 < CH - 1, pltpu.roll(b, CH - 1, 0), 1.0)
        rest = jnp.ones((CH, RC), F32)
        for i in reversed(range(ST)):
            rp[steps(i), :] = rest
            rest = rest * dp[steps(i), :]
        wait_all(factor_copies)
        before = jnp.ones((1, RC), F32)
        after = jnp.ones((1, RC), F32)
        for j in range(LINE):
            before = before * jnp.where(j < gi, abuf[j], 1.0)
            after = after * jnp.where(j > gi, abuf[j], 1.0)
        ends[2, 0:1, :] = before
        ends[3, 0:1, :] = after
        gabuf[gx] = before * after * abuf[gi]
        cross_copies = to_all(gabuf.at[gx], a2s, a2r, cross_peers)
        wait_all(table_copies)
        time_of = lax.broadcasted_iota(jnp.int32, (8, 128), 1)
        time_of = lax.rem(time_of, CH) * ST + time_of // CH
        for d in (1, 2):
            tabs[d] = jnp.where(tm + d < WINDOWS, tabs[d], DEAD)
        for d in range(3):
            local = lax.shift_right_arithmetic(tabs[d], 1) + (d - 2) * TW
            sel[8 * d : 8 * d + 8, :] = jnp.where(local == time_of, 1.0, 0.0)
        sel[24:32, :] = jnp.zeros((8, 128), F32)
        wait_all(cross_copies)

    def second_block(d):
        cell = lax.bitwise_and(tabs[d], 1) == 1
        return jnp.concatenate([cell] * (FB // 128), axis=1)

    copies = gather_start(xa, gas, gar)
    for c in load_spa:
        c.wait()
    gather_multiply(xa, gas, gar, copies, prepare)

    o = jnp.zeros((CH, RC), F32)
    for i in range(ST):
        o = dp[steps(i), :] * o + gp[steps(i), :] * mx[steps(i), :]
        mx[steps(i), :] = o
    for n, k in enumerate((1, 2, 4)):
        o = o + fstep[n] * jnp.where(sub8 >= k, pltpu.roll(o, k, 0), 0.0)
    bbuf[gi] = o[CH - 1 : CH, :]
    line_copies = to_all(bbuf.at[gi], bs, br, line_peers)
    entry = jnp.where(sub8 >= 1, pltpu.roll(o, 1, 0), 0.0)
    wait_all(line_copies)
    run = jnp.zeros((1, RC), F32)
    mine = run
    for j in range(LINE):
        mine = jnp.where(j == gi, run, mine)
        run = abuf[j] * run + bbuf[j]
    tbuf[gx] = run
    cross_copies = to_all(tbuf.at[gx], b2s, b2r, cross_peers)
    wait_all(cross_copies)
    run = jnp.zeros((1, RC), F32)
    for j in range(LINES):
        run = jnp.where(j < gx, gabuf[j] * run + tbuf[j], run)
    entry = entry + ends[0] * (mine + ends[2, 0:1, :] * run)
    for i in range(ST):
        mx[steps(i), :] = mx[steps(i), :] + fp[steps(i), :] * entry
    coarse = mx[...].astype(BF16)

    chosen = jnp.dot(sel[...].astype(BF16), coarse, preferred_element_type=F32)
    for d in range(3):
        rows = chosen[8 * d : 8 * d + 8, :]
        part = jnp.where(second_block(d), rows[:, FB:], rows[:, :FB])
        chs[3 + d if d else 0] = part
    row_copies = [send(chs.at[3 + d], chs.at[d], hs.at[d - 1], hr.at[d - 1], later[d - 1]) for d in (1, 2)]
    load_tiles.wait()
    wait_all(row_copies)
    picked = chs[0] + chs[1] + chs[2]

    sub_fb = lax.broadcasted_iota(jnp.int32, (8, FB), 0)
    seen = jnp.zeros((8, 128), F32)
    for s in range(SLOTS):
        lhs = jnp.where(sub_fb == tblock[0, 0, s], picked[s : s + 1, :], 0.0).astype(BF16)
        seen = seen + lax.dot_general(lhs, tiles[s], NT, preferred_element_type=F32)
    obs[r] = seen
    wait_all(to_all(obs.at[r], os_, or_, region_peers))
    observed = ((obs[0] + obs[1]) + obs[2]) + obs[3]
    weighted = (observed * noise[...]).astype(BF16).astype(F32)

    back = jnp.zeros((8, FB), F32)
    for s in range(SLOTS):
        row = jnp.sum(jnp.where(sub == tblock[0, 0, s], weighted, 0.0), axis=0, keepdims=True)
        lhs = jnp.where((sub == s) & (s < tcount[0, 0]), row, 0.0).astype(BF16)
        back = back + jnp.dot(lhs, tiles[s], preferred_element_type=F32)
    bks[0] = back
    wait_all([send(bks.at[0], bks.at[d], ks.at[d - 1], kr.at[d - 1], sooner[d - 1]) for d in (1, 2)])
    rows = []
    for d in range(3):
        second = second_block(d)
        rows.append(
            jnp.concatenate([jnp.where(second, 0.0, bks[d]), jnp.where(second, bks[d], 0.0)], axis=1)
        )
    rows.append(jnp.zeros((8, RC), F32))
    rows = jnp.concatenate(rows, axis=0)
    hot = sel[...].astype(BF16)
    first = rows.astype(BF16)
    left_over = rows - first.astype(F32)
    second = left_over.astype(BF16)
    third = (left_over - second.astype(F32)).astype(BF16)
    hx[...] = (
        lax.dot_general(hot, third, TN, preferred_element_type=F32)
        + lax.dot_general(hot, second, TN, preferred_element_type=F32)
    ) + lax.dot_general(hot, first, TN, preferred_element_type=F32)

    c = jnp.zeros((CH, RC), F32)
    for i in reversed(range(ST)):
        h = hx[steps(i), :] + c
        hx[steps(i), :] = h
        c = dp[steps(i), :] * h
    for n, k in enumerate((1, 2, 4)):
        c = c + bstep[n] * jnp.where(sub8 < CH - k, pltpu.roll(c, CH - k, 0), 0.0)
    cbuf[gi] = c[0:1, :]
    line_copies = to_all(cbuf.at[gi], cs, cr, line_peers)
    entry = jnp.where(sub8 < CH - 1, pltpu.roll(c, CH - 1, 0), 0.0)
    wait_all(line_copies)
    run = jnp.zeros((1, RC), F32)
    mine = run
    for j in reversed(range(LINE)):
        mine = jnp.where(j == gi, run, mine)
        run = abuf[j] * run + cbuf[j]
    ubuf[gx] = run
    wait_all(to_all(ubuf.at[gx], c2s, c2r, cross_peers))
    run = jnp.zeros((1, RC), F32)
    for j in reversed(range(LINES)):
        run = jnp.where(j > gx, gabuf[j] * run + ubuf[j], run)
    entry = entry + ends[1] * (mine + ends[3, 0:1, :] * run)
    for i in range(ST):
        held = hx[steps(i), :] + rp[steps(i), :] * entry
        hx[steps(i), :] = gp[steps(i), :] * held
    xb[0] = lax.dot_general(moved, hx[...].astype(BF16), TN, preferred_element_type=F32).astype(BF16)

    copies = gather_start(xb, gbs, gbr)

    def norms():
        load_res.wait()

    gather_multiply(xb, gbs, gbr, copies, norms)
    image = dirv[...] + mx[...]
    img[...] = image

    def whole(x):
        return jnp.sum(jnp.sum(x, axis=0, keepdims=True), axis=1, keepdims=True)

    def inverse(x):
        ok = x > 1e-37
        return jnp.where(ok, 1.0 / jnp.where(ok, x, 1.0), 0.0)

    res = resv[...]
    largest = jnp.max(jnp.max(jnp.abs(image), axis=0, keepdims=True), axis=1, keepdims=True)
    scaled = image * inverse(largest)
    stats = jnp.where(sub == 0, whole(res * res), 0.0)
    stats = jnp.where(sub == 1, whole(dirv[...] * image), stats)
    stats = jnp.where(sub == 2, whole(res * image), stats)
    stats = jnp.where(sub == 3, whole(scaled * scaled), stats)
    stats = jnp.where(sub == 4, largest, stats)

    def merged(buf, count):
        top = buf[0, 4:5, :]
        for j in range(1, count):
            top = jnp.maximum(top, buf[j, 4:5, :])
        inv = inverse(top)
        out = jnp.zeros((8, 128), F32)
        for j in range(count):
            scale = buf[j, 4:5, :] * inv
            out = out + jnp.where(sub == 3, buf[j] * (scale * scale), buf[j])
        return jnp.where(sub == 4, top, out)

    red1[gi] = stats
    wait_all(to_all(red1.at[gi], r1s, r1r, line_peers))
    here = gx * REGIONS + r
    red2[here] = merged(red1, LINE)
    wait_all(to_all(red2.at[here], r2s, r2r, plane_peers))
    stats = merged(red2, LINES * REGIONS)
    norm_old = stats[0:1, :]
    alpha = norm_old / stats[1:2, :]
    reach = alpha * stats[4:5, :]
    norm_new = jnp.maximum((norm_old - 2.0 * (alpha * stats[2:3, :])) + reach * (reach * stats[3:4, :]), 0.0)
    ab[...] = jnp.where(sub == 0, alpha, norm_new / norm_old)


def body(
    solution, residual, direction, decay, spatial, tiles,
    tile_block, tile_time, tile_cell, tile_count, noise_inv,
):
    any_spec = pl.BlockSpec(memory_space=pl.ANY)
    smem = pl.BlockSpec(memory_space=pltpu.SMEM)
    vmem = pl.BlockSpec(memory_space=pltpu.VMEM)
    vector = (1, RC)
    dma = pltpu.SemaphoreType.DMA
    sems = [7 + PIECES, 6, 6, 6, 6]
    for n in (LINE - 1, LINES - 1) * 3 + (2, 2, 2, REGIONS - 1, LINE - 1, LINES * REGIONS - 1):
        sems += [n, n]
    image, ab = pl.pallas_call(
        kernel,
        out_shape=(
            jax.ShapeDtypeStruct((TW, RC), F32),
            jax.ShapeDtypeStruct((8, 128), F32),
        ),
        in_specs=[any_spec] * 5 + [smem] * 4 + [vmem],
        out_specs=(vmem, vmem),
        scratch_shapes=[
            pltpu.VMEM((TW, RC), F32),
            pltpu.VMEM((TW, RC), F32),
            pltpu.VMEM((PIECES, TW, 128), F32),
            pltpu.VMEM((REGIONS, RC, RC), BF16),
            pltpu.VMEM((SLOTS, 128, FB), BF16),
            pltpu.VMEM((REGIONS, TW, RC), BF16),
            pltpu.VMEM((REGIONS, TW, RC), BF16),
            pltpu.VMEM((TW, RC), F32),
            pltpu.VMEM((TW, RC), F32),
            pltpu.VMEM((TW, RC), F32),
            pltpu.VMEM((TW, RC), F32),
            pltpu.VMEM((TW, RC), F32),
            pltpu.VMEM((TW, RC), F32),
            pltpu.VMEM((3, CH, RC), F32),
            pltpu.VMEM((3, CH, RC), F32),
            pltpu.VMEM((4, CH, RC), F32),
            pltpu.VMEM((LINE,) + vector, F32),
            pltpu.VMEM((LINES,) + vector, F32),
            pltpu.VMEM((LINE,) + vector, F32),
            pltpu.VMEM((LINES,) + vector, F32),
            pltpu.VMEM((LINE,) + vector, F32),
            pltpu.VMEM((LINES,) + vector, F32),
            pltpu.VMEM((3, 8, 128), jnp.int32),
            pltpu.VMEM((6, 8, FB), F32),
            pltpu.VMEM((3, 8, FB), F32),
            pltpu.VMEM((REGIONS, 8, 128), F32),
            pltpu.VMEM((LINE, 8, 128), F32),
            pltpu.VMEM((LINES * REGIONS, 8, 128), F32),
            pltpu.VMEM((32, 128), F32),
        ]
        + [dma((n,)) for n in sems],
        compiler_params=pltpu.CompilerParams(
            collective_id=0, has_side_effects=True, vmem_limit_bytes=48 << 20
        ),
        cost_estimate=pl.CostEstimate(
            flops=4 * TW * RC * RC * REGIONS, bytes_accessed=12 << 20, transcendentals=TW * RC
        ),
        name="cg_step",
    )(direction, residual, decay, spatial, tiles, tile_block, tile_time, tile_cell, tile_count, noise_inv)
    alpha = ab[0, 0]
    beta = ab[1, 0]
    residual_new = residual - alpha * image
    return (solution + alpha * direction, residual_new, residual_new + beta * direction)


def solution(mesh):
    return jax.shard_map(
        body,
        mesh=mesh,
        in_specs=(
            P("tm", "region"),
            P("tm", "region"),
            P("tm", "region"),
            P("tm", "region"),
            P("region", None),
            P("tm", "region", None, None, None),
            P("tm", "region", None),
            P("tm", "region", None),
            P("tm", "region", None),
            P("tm", "region"),
            P("tm", None),
        ),
        out_specs=(P("tm", "region"), P("tm", "region"), P("tm", "region")),
        check_vma=False,
    )
```

time: 655 us -> 90.4 us (0.14); the launches traced: 648 us -> 90.1 us
  blocking collectives: 379 us -> 0 us
  local copies, waits for them, and re-layouts: 123 us -> 7.58 us
  Pallas kernels: 0 us -> 78.7 us
  waiting for transfers between devices: 62 us -> 0 us
  other arithmetic: 36.4 us -> 2.54 us
  between operations: 18.7 us -> 1.31 us
  matrix products: 14.4 us -> 0 us
  starting transfers between devices: 13 us -> 0 us
    all_gather x4 -> x0, blocking collectives: 221 us -> none  [carried_in(): gathered = jax.tree.map(lambda a: lax.all_gather(a, axis), part)]
    psum x3 -> x0, blocking collectives: 158 us -> none  [the longest x1 76 us: body(): norm_old = lax.psum(jnp.sum(residual * residual), ('tm', 'region'))]
    pallas_call x0 -> x1, Pallas kernels: none -> 78.7 us  [body(): pl.pallas_call(kernel, out_shape=(jax.ShapeDtypeStruct((TW, RC), F32), ja...]
    dynamic_slice x63 -> x0, local copies, waits for them, and re-layouts: 48.6 us -> none  [one(): lax.dynamic_index_in_dim(a, source, 0, False)]
    slice x98 -> x1, local copies, waits for them, and re-layouts: 46.5 us -> 0.58 us  [body(): beta = ab[1, 0]]
    all_gather x1 -> x0, waiting for transfers between devices: 25.8 us -> none  [body(): lax.all_gather(dir_half, 'region', axis=1, tiled=True)]
    reduce_scatter x1 -> x0, waiting for transfers between devices: 22.9 us -> none  [body(): lax.psum_scatter(contribution, 'region', scatter_dimension=1, tiled=True)]
    pad x48 -> x0, local copies, waits for them, and re-layouts: 17.5 us -> none  [the longest x24 9.22 us: body(): lax.associative_scan(compose, (decay, decay * adjoint), reverse=True, axi...]
  transfers between devices with their start and end apart: 6 -> 0, of which waited for: 5 -> 0; matrix products, arithmetic and copies ran while one was open for 2% -> 0% of each run, Pallas kernels for 0% -> 0%
where the time goes in v1:
time: 90.4 us; the launch traced here: 90.1 us
  Pallas kernels  78.7 us (87%)
  local copies, waits for them, and re-layouts  7.58 us (8%)
  other arithmetic  2.54 us (3%)
  between operations  1.31 us (1%)
    pallas_call x1, Pallas kernels, body(): pl.pallas_call(kernel, out_shape=(jax.ShapeDtypeStruct((TW, RC), F32), ja...  78.7 us
    unnamed x18, local copies, waits for them, and re-layouts  7 us
    add x1, other arithmetic, body(): residual_new + beta * direction  2.54 us

profile of v1, /device:TPU:1, one launch (start us, length us, event | category | flops | bytes accessed | tf_op | source)
XLA Modules:
  0.0 90.1 jit_solution(15847171397066284953)
XLA Ops:
  1.3 0.0 copy-start
  1.3 1.0 %copy-done = f32[128,1024]{1,0:T(8,128)S(1)} copy-done((f32[128,1024]{1,0:T(8,128)S(1)}, f32[128,1024]{1,0:T(8,128)}, u32[]{:S(2)}) %copy-start) | copy-done | bytes 524312
  2.3 0.0 copy-start.1
  2.3 1.0 %copy-done.1 = f32[128,1024]{1,0:T(8,128)S(1)} copy-done((f32[128,1024]{1,0:T(8,128)S(1)}, f32[128,1024]{1,0:T(8,128)}, u32[]{:S(2)}) %copy-start.1) | copy-done | bytes 524312
  3.4 0.0 copy-start.2
  3.4 1.2 %copy-done.2 = bf16[1,1,8,128,512]{4,3,2,1,0:T(8,128)(2,1)S(1)} copy-done((bf16[1,1,8,128,512]{4,3,2,1,0:T(8,128)(2,1)S(1)}, bf16[1,1,8,128,512]{4,3,2,1,0:T(8,128)(2,1)}, u32[]{:S(2)}) %copy-start.2) | copy-done | bytes 1048600
  4.6 0.0 copy-start.3
  4.6 1.0 %copy-done.3 = f32[128,1024]{1,0:T(8,128)S(1)} copy-done((f32[128,1024]{1,0:T(8,128)S(1)}, f32[128,1024]{1,0:T(8,128)}, u32[]{:S(2)}) %copy-start.3) | copy-done | bytes 524312
  5.6 0.0 copy-start.4
  5.6 0.7 copy-done.4
  6.3 0.0 copy-start.5
  6.3 0.7 copy-done.5
  7.0 0.0 copy-start.6
  7.0 0.7 copy-done.6
  7.6 0.0 copy-start.7
  7.6 0.7 copy-done.7
  8.3 0.0 copy-start.8
  8.3 78.7 %cg_step.1 = (f32[128,1024]{1,0:T(8,128)S(1)}, f32[8,128]{1,0:T(8,128)S(1)}) custom-call(f32[128,1024]{1,0:T(8,128)S(1)} %copy-done, f32[128,1024]{1,0:T(8,128)S(1)} %copy-done.1, f32[128,1024]{1,0:T(8,128)S(1)} %copy-done.3, bf16[1024,4096]{1,0:T(8,128)(2,1)} %spa_h.1, bf16[1,1,8,128,512]{4,3,2,1,0:T(8,128)(2,1)S(1)} %copy-done.2, ...), custom_call_target="tpu_custom_call" | custom-call | flops 2147483648 | bytes 12582912 | tf_op jit(solution)/shard_map/cg_step/pallas_call | solution.py:365
  87.0 0.6 fusion
  87.6 0.0 copy-done.8
  87.6 2.5 %multiply_add_fusion = (f32[128,1024]{1,0:T(8,128)}, f32[128,1024]{1,0:T(8,128)}, f32[128,1024]{1,0:T(8,128)}) fusion(f32[128,1024]{1,0:T(8,128)S(1)} %copy-done, f32[]{:T(128)} %bitcast.1, f32[128,1024]{1,0:T(8,128)S(1)} %copy-done.1, f32[128,1024]{1,0:T(8,128)S(1)} %get-tuple-element.6, f32[]{:T(128)} %bitcast, f32[128,1024]{1,0:T(8,128)S(1)} %copy-done.8), kind=kLoop, calls=%fused_computation | loop fusion | flops 786432 | bytes 3670024 | tf_op jit(solution)/shard_map/add | solution.py:416
Async XLA Ops:
  1.3 1.0 %copy-start = (f32[128,1024]{1,0:T(8,128)S(1)}, f32[128,1024]{1,0:T(8,128)}, u32[]{:S(2)}) copy-start(f32[128,1024]{1,0:T(8,128)} %dir_h.1) | copy-start | bytes 1572868
  2.3 1.0 %copy-start.1 = (f32[128,1024]{1,0:T(8,128)S(1)}, f32[128,1024]{1,0:T(8,128)}, u32[]{:S(2)}) copy-start(f32[128,1024]{1,0:T(8,128)} %res_h.1) | copy-start | bytes 1572868
  3.4 1.2 %copy-start.2 = (bf16[1,1,8,128,512]{4,3,2,1,0:T(8,128)(2,1)S(1)}, bf16[1,1,8,128,512]{4,3,2,1,0:T(8,128)(2,1)}, u32[]{:S(2)}) copy-start(bf16[1,1,8,128,512]{4,3,2,1,0:T(8,128)(2,1)} %tiles_h.1) | copy-start | bytes 3145732
  4.6 1.0 %copy-start.3 = (f32[128,1024]{1,0:T(8,128)S(1)}, f32[128,1024]{1,0:T(8,128)}, u32[]{:S(2)}) copy-start(f32[128,1024]{1,0:T(8,128)} %dec_h.1) | copy-start | bytes 1572868
  5.6 0.7 copy-start.4
  6.3 0.7 copy-start.5
  7.0 0.7 copy-start.6
  7.6 0.7 copy-start.7
  8.3 79.3 %copy-start.8 = (f32[128,1024]{1,0:T(8,128)S(1)}, f32[128,1024]{1,0:T(8,128)}, u32[]{:S(2)}) copy-start(f32[128,1024]{1,0:T(8,128)} %param.11) | copy-start | bytes 1572868

commit v2 on v1

v2 whole, which is shorter than its diff:
```python
import jax
import jax.numpy as jnp
from jax import lax
from jax.experimental import pallas as pl
from jax.experimental.pallas import tpu as pltpu
from jax.sharding import PartitionSpec as P

MESH = pl.DeviceIdType.MESH
TW = 128
RC = 1024
FB = 512
SLOTS = 8
LINE = 16
LINES = 4
REGIONS = 4
WINDOWS = LINE * LINES
CH = 8
ST = TW // CH
PIECES = RC // 128
DEAD = -8192
F32 = jnp.float32
BF16 = jnp.bfloat16
NT = (((1,), (1,)), ((), ()))
TN = (((0,), (0,)), ((), ()))


def kernel(
    dir_h, res_h, dec_h, spa_h, tiles_h, tblock_h, ttime_h, tcell_h, tcount_h, noise_h,
    img, alpha_o, beta_o,
    tblock, ttime, tcell, tcount, noise,
    imgv, dirv, resv, decv, spa, tiles, xa, xb, dp, gp, fp, rp, mx, hx, fstep, bstep, ends,
    abuf, gabuf, bbuf, tbuf, cbuf, ubuf, tabs, chs, ffs, bks, near, obs, red1, red2, sel,
    lsem, gas, gar, gbs, gbr, as_, ar, a2s, a2r, bs, br, b2s, b2r, cs, cr, c2s, c2r,
    ts, tr, hs, hr, fs, fr, ks, kr, ns, nr, os_, or_, r1s, r1r, r2s, r2r,
):
    tm = lax.axis_index("tm")
    r = lax.axis_index("region")
    gx = tm // LINE
    gi = lax.rem(tm, LINE)

    loads = [pltpu.make_async_copy(dir_h, dirv, lsem.at[0])]
    for k in range(REGIONS):
        src = lax.rem(r + REGIONS - k, REGIONS)
        cols = pl.ds(pl.multiple_of(src * RC, RC), RC)
        loads.append(pltpu.make_async_copy(spa_h.at[:, cols], spa.at[k], lsem.at[1 + k]))
    loads.append(pltpu.make_async_copy(tiles_h.at[0, 0], tiles, lsem.at[5]))
    loads.append(pltpu.make_async_copy(res_h, resv, lsem.at[6]))
    for n in range(PIECES):
        loads.append(pltpu.make_async_copy(dec_h.at[:, 128 * n : 128 * (n + 1)], decv.at[n], lsem.at[7 + n]))
    small = ((tcount_h, tcount), (ttime_h, ttime), (tcell_h, tcell), (tblock_h, tblock), (noise_h, noise))
    for n, (there, here) in enumerate(small):
        loads.append(pltpu.make_async_copy(there, here, lsem.at[7 + PIECES + n]))
    load_small = loads[7 + PIECES :]
    load_dir, load_spa, load_tiles, load_res, load_dec = loads[0], loads[1:5], loads[5], loads[6], loads[7 : 7 + PIECES]
    for c in loads:
        c.start()

    line_peers = [(gx * LINE + lax.rem(gi + k, LINE), r) for k in range(1, LINE)]
    cross_peers = [(lax.rem(gx + k, LINES) * LINE + gi, r) for k in range(1, LINES)]
    region_peers = [(tm, lax.rem(r + k, REGIONS)) for k in range(1, REGIONS)]
    plane_peers = [
        (lax.rem(gx + kx, LINES) * LINE + gi, lax.rem(r + ky, REGIONS))
        for kx in range(LINES)
        for ky in range(REGIONS)
        if kx or ky
    ]
    later = [(lax.rem(tm + d, WINDOWS), r) for d in (1, 2)]
    sooner = [(lax.rem(tm + WINDOWS - d, WINDOWS), r) for d in (1, 2)]

    barrier = pltpu.get_barrier_semaphore()
    everyone = line_peers + plane_peers + later + sooner
    for peer in everyone:
        pl.semaphore_signal(barrier, inc=1, device_id=peer, device_id_type=MESH)

    sent = []

    def send(src, dst, ss, rs, peer):
        c = pltpu.make_async_remote_copy(
            src_ref=src, dst_ref=dst, send_sem=ss, recv_sem=rs, device_id=peer, device_id_type=MESH
        )
        c.start()
        sent.append(c)
        return c

    def to_all(ref, ss, rs, peers):
        return [send(ref, ref, ss.at[k], rs.at[k], peer) for k, peer in enumerate(peers)]

    def received(copies):
        for c in copies:
            c.wait_recv()

    sub8 = lax.broadcasted_iota(jnp.int32, (CH, RC), 0)
    sub = lax.broadcasted_iota(jnp.int32, (8, 128), 0)

    load_dir.wait()
    row = lax.broadcasted_iota(jnp.int32, (TW, TW), 0)
    col = lax.broadcasted_iota(jnp.int32, (TW, TW), 1)
    moved = jnp.where(lax.rem(row, CH) * ST + row // CH == col, 1.0, 0.0).astype(BF16)
    xa[0] = jnp.dot(moved, dirv[...].astype(BF16), preferred_element_type=F32).astype(BF16)

    pl.semaphore_wait(barrier, len(everyone))

    low, high = pl.ds(0, TW // 2), pl.ds(TW // 2, TW // 2)
    right = (tm, lax.rem(r + 1, REGIONS))
    left = (tm, lax.rem(r + REGIONS - 1, REGIONS))

    def gather_start(x, ss, rs):
        return [
            send(x.at[0, low], x.at[1, low], ss.at[0], rs.at[0], right),
            send(x.at[0, high], x.at[3, high], ss.at[1], rs.at[1], left),
            send(x.at[0, high], x.at[1, high], ss.at[2], rs.at[2], right),
            send(x.at[0, low], x.at[3, low], ss.at[3], rs.at[3], left),
        ]

    def gather_pass(x, ss, rs, copies):
        copies[0].wait_recv()
        copies.append(send(x.at[1, low], x.at[2, low], ss.at[4], rs.at[4], right))
        copies[1].wait_recv()
        copies.append(send(x.at[3, high], x.at[2, high], ss.at[5], rs.at[5], left))

    def multiply(x, k, first):
        def tile(n, _):
            cols = pl.ds(pl.multiple_of(n * 256, 256), 256)
            part = lax.dot_general(x[k], spa[k, cols, :], NT, preferred_element_type=F32)
            if first:
                mx[:, cols] = part
            else:
                mx[:, cols] += part
            return 0

        lax.fori_loop(0, RC // 256, tile, 0)

    def steps(i):
        return slice(CH * i, CH * (i + 1))

    def thirds(x):
        first = x.astype(BF16)
        left_over = x - first.astype(F32)
        second = left_over.astype(BF16)
        return first, second, (left_over - second.astype(F32)).astype(BF16)

    def second_block(d):
        cell = lax.bitwise_and(tabs[d], 1) == 1
        return jnp.concatenate([cell] * (FB // 128), axis=1)

    def hand_on(dense, buf, ss, rs):
        first, second, third = thirds(dense)
        hot = sel[...].astype(BF16)
        rows = (
            jnp.dot(hot, third, preferred_element_type=F32) + jnp.dot(hot, second, preferred_element_type=F32)
        ) + jnp.dot(hot, first, preferred_element_type=F32)
        for d in range(3):
            part = rows[8 * d : 8 * d + 8, :]
            buf[2 + d if d else 0] = jnp.where(second_block(d), part[:, FB:], part[:, :FB])
        return [send(buf.at[2 + d], buf.at[d], ss.at[d - 1], rs.at[d - 1], later[d - 1]) for d in (1, 2)]

    copies = gather_start(xa, gas, gar)

    for load in load_small:
        load.wait()
    table = jnp.full((8, 128), DEAD, jnp.int32)
    for s in range(SLOTS):
        key = jnp.where(s < tcount[0, 0], ttime[0, 0, s] * 2 + tcell[0, 0, s], DEAD)
        table = jnp.where(sub == s, key, table)
    tabs[0] = table
    table_copies = [
        send(tabs.at[0], tabs.at[d], ts.at[d - 1], tr.at[d - 1], sooner[d - 1]) for d in (1, 2)
    ]
    for load in load_dec:
        load.wait()
    f = jnp.ones((CH, RC), F32)
    for i in range(ST):
        d = jnp.concatenate([decv[n, pl.ds(i, CH, stride=ST), :] for n in range(PIECES)], axis=1)
        dp[steps(i), :] = d
        f = f * d
        fp[steps(i), :] = f
    total = f
    for n, k in enumerate((1, 2, 4)):
        fstep[n] = f
        f = f * jnp.where(sub8 >= k, pltpu.roll(f, k, 0), 1.0)
    abuf[gi] = f[CH - 1 : CH, :]
    factor_copies = to_all(abuf.at[gi], as_, ar, line_peers)
    chunk_before = jnp.where(sub8 >= 1, pltpu.roll(f, 1, 0), 1.0)
    for i in range(ST):
        hx[steps(i), :] = fp[steps(i), :] * chunk_before
    b = total
    for n, k in enumerate((1, 2, 4)):
        bstep[n] = b
        b = b * jnp.where(sub8 < CH - k, pltpu.roll(b, CH - k, 0), 1.0)
    ends[1] = jnp.where(sub8 < CH - 1, pltpu.roll(b, CH - 1, 0), 1.0)

    received(table_copies)
    time_of = lax.broadcasted_iota(jnp.int32, (8, 128), 1)
    time_of = lax.rem(time_of, CH) * ST + time_of // CH
    for d in (1, 2):
        tabs[d] = jnp.where(tm + d < WINDOWS, tabs[d], DEAD)
    for d in range(3):
        local = lax.shift_right_arithmetic(tabs[d], 1) + (d - 2) * TW
        sel[8 * d : 8 * d + 8, :] = jnp.where(local == time_of, 1.0, 0.0)
    sel[24:32, :] = jnp.zeros((8, 128), F32)
    factor_rows = hand_on(hx[...], ffs, fs, fr)
    gather_pass(xa, gas, gar, copies)
    for load in load_spa:
        load.wait()

    multiply(xa, 0, True)
    received(factor_copies)
    run = jnp.ones((1, RC), F32)
    places = [run] * 3
    for j in range(LINE):
        for n in range(3):
            places[n] = jnp.where(j == gi - n, run, places[n])
        if j >= LINE - 2:
            gabuf[gx, LINE - j] = run
        run = run * abuf[j]
    gabuf[gx, 0] = run
    gabuf[gx, 3] = abuf[LINE - 1]
    gabuf[gx, 4] = abuf[LINE - 2]
    cross_copies = to_all(gabuf.at[gx], a2s, a2r, cross_peers)
    for n in range(3):
        ends[2, n : n + 1, :] = places[n]
    run = jnp.ones((1, RC), F32)
    for j in range(3, LINE):
        run = run * jnp.where(j >= gi + 3, abuf[j - 2], 1.0)
    ends[3, 0:1, :] = run
    rest = jnp.ones((CH, RC), F32)
    for i in reversed(range(ST)):
        d = dp[steps(i), :]
        gp[steps(i), :] = jnp.sqrt(1.0 - d * d)
        rp[steps(i), :] = rest
        rest = rest * d
    received(copies[2:3])
    multiply(xa, 1, False)
    received(copies[3:4])
    multiply(xa, 3, False)
    received(copies[4:6])
    multiply(xa, 2, False)

    o = jnp.zeros((CH, RC), F32)
    for i in range(ST):
        o = dp[steps(i), :] * o + gp[steps(i), :] * mx[steps(i), :]
        mx[steps(i), :] = o
    for n, k in enumerate((1, 2, 4)):
        o = o + fstep[n] * jnp.where(sub8 >= k, pltpu.roll(o, k, 0), 0.0)
    bbuf[gi] = o[CH - 1 : CH, :]
    line_copies = to_all(bbuf.at[gi], bs, br, line_peers)

    entry = jnp.where(sub8 >= 1, pltpu.roll(o, 1, 0), 0.0)
    for i in range(ST):
        mx[steps(i), :] = mx[steps(i), :] + fp[steps(i), :] * entry
    row_copies = hand_on(mx[...], chs, hs, hr)
    received(cross_copies)
    received(factor_rows)
    before = lax.rem(gx + LINES - 1, LINES)
    ends[3, 1:2, :] = jnp.where(gi >= 1, abuf[lax.rem(gi + LINE - 1, LINE)], gabuf[before, 3])
    ends[3, 2:3, :] = jnp.where(
        gi >= 2, abuf[lax.rem(gi + LINE - 2, LINE)], jnp.where(gi == 1, gabuf[before, 3], gabuf[before, 4])
    )
    received(line_copies)
    run = jnp.zeros((1, RC), F32)
    places = [run] * 3
    for j in range(LINE):
        for n in range(3):
            places[n] = jnp.where(j == gi - n, run, places[n])
        if j >= LINE - 2:
            tbuf[gx, LINE - j] = run
        run = abuf[j] * run + bbuf[j]
    tbuf[gx, 0] = run
    cross_copies = to_all(tbuf.at[gx], b2s, b2r, cross_peers)
    received(row_copies)
    received(cross_copies)
    run = jnp.zeros((1, RC), F32)
    line_before = run
    for j in range(LINES):
        line_before = jnp.where(j == gx - 1, run, line_before)
        run = jnp.where(j < gx, gabuf[j, 0] * run + tbuf[j, 0], run)
    last, last_but = [tbuf[before, n] + gabuf[before, n] * line_before for n in (1, 2)]
    inside = [places[n] + ends[2, n : n + 1, :] * run for n in range(3)]
    entering = [
        inside[0],
        jnp.where(gi >= 1, inside[1], last),
        jnp.where(gi >= 2, inside[2], jnp.where(gi == 1, last, last_but)),
    ]
    own_second = second_block(0)
    picked = jnp.zeros((8, FB), F32)
    for d in range(3):
        state = jnp.where(own_second, entering[d][:, FB:], entering[d][:, :FB])
        picked = picked + (chs[d] + ffs[d] * state)
    load_tiles.wait()

    sub_fb = lax.broadcasted_iota(jnp.int32, (8, FB), 0)
    seen = jnp.zeros((8, 128), F32)
    for s in range(SLOTS):
        lhs = jnp.where(sub_fb == tblock[0, 0, s], picked[s : s + 1, :], 0.0).astype(BF16)
        seen = seen + lax.dot_general(lhs, tiles[s], NT, preferred_element_type=F32)
    obs[r] = seen
    received(to_all(obs.at[r], os_, or_, region_peers))
    observed = ((obs[0] + obs[1]) + obs[2]) + obs[3]
    weighted = (observed * noise[...]).astype(BF16).astype(F32)

    back = jnp.zeros((8, FB), F32)
    for s in range(SLOTS):
        row = jnp.sum(jnp.where(sub == tblock[0, 0, s], weighted, 0.0), axis=0, keepdims=True)
        lhs = jnp.where((sub == s) & (s < tcount[0, 0]), row, 0.0).astype(BF16)
        back = back + jnp.dot(lhs, tiles[s], preferred_element_type=F32)
    bks[0] = back

    adds = []
    for d in range(3):
        term = ffs[d] * back
        adds.append(
            jnp.concatenate(
                [
                    jnp.sum(jnp.where(own_second, 0.0, term), axis=0, keepdims=True),
                    jnp.sum(jnp.where(own_second, term, 0.0), axis=0, keepdims=True),
                ],
                axis=1,
            )
        )
    one_down = adds[1] + ends[3, 1:2, :] * adds[0]
    cbuf[gi] = adds[2] + ends[3, 2:3, :] * one_down
    line_copies = to_all(cbuf.at[gi], cs, cr, line_peers)
    near[2] = adds[0]
    near[3] = one_down
    near_copies = [send(near.at[1 + d], near.at[d - 1], ns.at[d - 1], nr.at[d - 1], sooner[d - 1]) for d in (1, 2)]
    row_copies = [send(bks.at[0], bks.at[d], ks.at[d - 1], kr.at[d - 1], sooner[d - 1]) for d in (1, 2)]
    received(row_copies)
    rows = []
    for d in range(3):
        second = second_block(d)
        rows.append(
            jnp.concatenate([jnp.where(second, 0.0, bks[d]), jnp.where(second, bks[d], 0.0)], axis=1)
        )
    rows.append(jnp.zeros((8, RC), F32))
    first, second, third = thirds(jnp.concatenate(rows, axis=0))
    hot = sel[...].astype(BF16)
    hx[...] = (
        lax.dot_general(hot, third, TN, preferred_element_type=F32)
        + lax.dot_general(hot, second, TN, preferred_element_type=F32)
    ) + lax.dot_general(hot, first, TN, preferred_element_type=F32)

    c = jnp.zeros((CH, RC), F32)
    for i in reversed(range(ST)):
        h = hx[steps(i), :] + c
        hx[steps(i), :] = h
        c = dp[steps(i), :] * h
    for n, k in enumerate((1, 2, 4)):
        c = c + bstep[n] * jnp.where(sub8 < CH - k, pltpu.roll(c, CH - k, 0), 0.0)
    entry = jnp.where(sub8 < CH - 1, pltpu.roll(c, CH - 1, 0), 0.0)
    received(near_copies)
    close = jnp.where(tm + 1 < WINDOWS, near[0], 0.0) + jnp.where(tm + 2 < WINDOWS, near[1], 0.0)
    received(line_copies)
    run = jnp.zeros((1, RC), F32)
    for j in reversed(range(2, LINE)):
        run = abuf[j - 2] * run + cbuf[j]
    ubuf[gx, 0] = run
    ubuf[gx, 1] = cbuf[1]
    ubuf[gx, 2] = cbuf[0]
    cross_copies = to_all(ubuf.at[gx], c2s, c2r, cross_peers)
    mine = jnp.zeros((1, RC), F32)
    for j in reversed(range(3, LINE)):
        mine = jnp.where(j >= gi + 3, abuf[j - 2] * mine + cbuf[j], mine)
    received(cross_copies)
    zero = jnp.zeros((1, RC), F32)
    two, one, run = zero, zero, zero
    for j in reversed(range(1, LINES)):
        above = j > gx
        two = jnp.where(above, ubuf[j, 0] + gabuf[j, 2] * run, two)
        one = jnp.where(above, gabuf[j - 1, 3] * two + ubuf[j, 1], one)
        run = jnp.where(above, gabuf[j - 1, 4] * one + ubuf[j, 2], run)
    far = jnp.where(gi == LINE - 1, two, jnp.where(gi == LINE - 2, one, mine + ends[3, 0:1, :] * run))
    entry = entry + ends[1] * (close + far)
    for i in range(ST):
        held = hx[steps(i), :] + rp[steps(i), :] * entry
        hx[steps(i), :] = gp[steps(i), :] * held
    xb[0] = lax.dot_general(moved, hx[...].astype(BF16), TN, preferred_element_type=F32).astype(BF16)

    copies = gather_start(xb, gbs, gbr)

    gather_pass(xb, gbs, gbr, copies)
    multiply(xb, 0, True)
    received(copies[2:3])
    multiply(xb, 1, False)
    received(copies[3:4])
    multiply(xb, 3, False)
    load_res.wait()
    received(copies[4:6])
    multiply(xb, 2, False)

    image = dirv[...] + mx[...]
    imgv[...] = image
    store = pltpu.make_async_copy(imgv, img, lsem.at[12 + PIECES])
    store.start()

    def whole(x):
        return jnp.sum(jnp.sum(x, axis=0, keepdims=True), axis=1, keepdims=True)

    def inverse(x):
        ok = x > 1e-37
        return jnp.where(ok, 1.0 / jnp.where(ok, x, 1.0), 0.0)

    res = resv[...]
    largest = jnp.max(jnp.max(jnp.abs(image), axis=0, keepdims=True), axis=1, keepdims=True)
    scaled = image * inverse(largest)
    stats = jnp.where(sub == 0, whole(res * res), 0.0)
    stats = jnp.where(sub == 1, whole(dirv[...] * image), stats)
    stats = jnp.where(sub == 2, whole(res * image), stats)
    stats = jnp.where(sub == 3, whole(scaled * scaled), stats)
    stats = jnp.where(sub == 4, largest, stats)

    def merged(buf, count):
        top = buf[0, 4:5, :]
        for j in range(1, count):
            top = jnp.maximum(top, buf[j, 4:5, :])
        inv = inverse(top)
        out = jnp.zeros((8, 128), F32)
        for j in range(count):
            scale = buf[j, 4:5, :] * inv
            out = out + jnp.where(sub == 3, buf[j] * (scale * scale), buf[j])
        return jnp.where(sub == 4, top, out)

    red1[gi] = stats
    received(to_all(red1.at[gi], r1s, r1r, line_peers))
    here = gx * REGIONS + r
    red2[here] = merged(red1, LINE)
    received(to_all(red2.at[here], r2s, r2r, plane_peers))
    stats = merged(red2, LINES * REGIONS)
    norm_old = stats[0:1, :]
    alpha = norm_old / stats[1:2, :]
    reach = alpha * stats[4:5, :]
    norm_new = jnp.maximum((norm_old - 2.0 * (alpha * stats[2:3, :])) + reach * (reach * stats[3:4, :]), 0.0)
    alpha_o[...] = alpha[:, 0:1]
    beta_o[...] = (norm_new / norm_old)[:, 0:1]
    store.wait()
    for c in sent:
        c.wait_send()


def body(
    solution, residual, direction, decay, spatial, tiles,
    tile_block, tile_time, tile_cell, tile_count, noise_inv,
):
    hbm = pl.BlockSpec(memory_space=pltpu.HBM)
    vmem = pl.BlockSpec(memory_space=pltpu.VMEM)
    vector = (1, RC)
    dma = pltpu.SemaphoreType.DMA
    sems = [13 + PIECES, 6, 6, 6, 6]
    for n in (LINE - 1, LINES - 1) * 3 + (2, 2, 2, 2, 2, REGIONS - 1, LINE - 1, LINES * REGIONS - 1):
        sems += [n, n]
    image, alpha, beta = pl.pallas_call(
        kernel,
        out_shape=(
            jax.ShapeDtypeStruct((TW, RC), F32),
            jax.ShapeDtypeStruct((1, 1), F32),
            jax.ShapeDtypeStruct((1, 1), F32),
        ),
        in_specs=[hbm] * 10,
        out_specs=(hbm, vmem, vmem),
        scratch_shapes=[
            pltpu.SMEM((1, 1, SLOTS), jnp.int32),
            pltpu.SMEM((1, 1, SLOTS), jnp.int32),
            pltpu.SMEM((1, 1, SLOTS), jnp.int32),
            pltpu.SMEM((1, 1), jnp.int32),
            pltpu.VMEM((8, 128), F32),
            pltpu.VMEM((TW, RC), F32),
            pltpu.VMEM((TW, RC), F32),
            pltpu.VMEM((TW, RC), F32),
            pltpu.VMEM((PIECES, TW, 128), F32),
            pltpu.VMEM((REGIONS, RC, RC), BF16),
            pltpu.VMEM((SLOTS, 128, FB), BF16),
            pltpu.VMEM((REGIONS, TW, RC), BF16),
            pltpu.VMEM((REGIONS, TW, RC), BF16),
            pltpu.VMEM((TW, RC), F32),
            pltpu.VMEM((TW, RC), F32),
            pltpu.VMEM((TW, RC), F32),
            pltpu.VMEM((TW, RC), F32),
            pltpu.VMEM((TW, RC), F32),
            pltpu.VMEM((TW, RC), F32),
            pltpu.VMEM((3, CH, RC), F32),
            pltpu.VMEM((3, CH, RC), F32),
            pltpu.VMEM((4, CH, RC), F32),
            pltpu.VMEM((LINE,) + vector, F32),
            pltpu.VMEM((LINES, 5) + vector, F32),
            pltpu.VMEM((LINE,) + vector, F32),
            pltpu.VMEM((LINES, 3) + vector, F32),
            pltpu.VMEM((LINE,) + vector, F32),
            pltpu.VMEM((LINES, 3) + vector, F32),
            pltpu.VMEM((3, 8, 128), jnp.int32),
            pltpu.VMEM((5, 8, FB), F32),
            pltpu.VMEM((5, 8, FB), F32),
            pltpu.VMEM((3, 8, FB), F32),
            pltpu.VMEM((4,) + vector, F32),
            pltpu.VMEM((REGIONS, 8, 128), F32),
            pltpu.VMEM((LINE, 8, 128), F32),
            pltpu.VMEM((LINES * REGIONS, 8, 128), F32),
            pltpu.VMEM((32, 128), F32),
        ]
        + [dma((n,)) for n in sems],
        compiler_params=pltpu.CompilerParams(
            collective_id=0, has_side_effects=True, vmem_limit_bytes=62 << 20
        ),
        cost_estimate=pl.CostEstimate(
            flops=4 * TW * RC * RC * REGIONS, bytes_accessed=12 << 20, transcendentals=TW * RC
        ),
        name="cg_step",
    )(direction, residual, decay, spatial, tiles, tile_block, tile_time, tile_cell, tile_count, noise_inv)
    alpha = alpha[0, 0]
    beta = beta[0, 0]
    residual_new = residual - alpha * image
    return (solution + alpha * direction, residual_new, residual_new + beta * direction)


def solution(mesh):
    return jax.shard_map(
        body,
        mesh=mesh,
        in_specs=(
            P("tm", "region"),
            P("tm", "region"),
            P("tm", "region"),
            P("tm", "region"),
            P("region", None),
            P("tm", "region", None, None, None),
            P("tm", "region", None),
            P("tm", "region", None),
            P("tm", "region", None),
            P("tm", "region"),
            P("tm", None),
        ),
        out_specs=(P("tm", "region"), P("tm", "region"), P("tm", "region")),
        check_vma=False,
    )
```

time: 90.4 us -> 74 us (0.82)
  Pallas kernels: 78.7 us -> 68.7 us
  local copies, waits for them, and re-layouts: 7.58 us -> 0.01 us
  other arithmetic: 2.54 us -> 3.71 us
    pallas_call x1, Pallas kernels: 78.7 us -> 68.7 us  [body(): pl.pallas_call(kernel, out_shape=(jax.ShapeDtypeStruct((TW, RC), F32), ja...]
    unnamed x18 -> x6, local copies, waits for them, and re-layouts: 7 us -> 0.01 us
    add x1, other arithmetic: 2.54 us -> 3.71 us  [body(): residual_new + beta * direction]
where the time goes in v2:
time: 74 us; the launch traced here: 73.9 us
  Pallas kernels  68.7 us (93%)
  other arithmetic  3.71 us (5%)
  between operations  1.45 us (2%)
    pallas_call x1, Pallas kernels, body(): pl.pallas_call(kernel, out_shape=(jax.ShapeDtypeStruct((TW, RC), F32), ja...  68.7 us
    add x1, other arithmetic, body(): residual_new + beta * direction  3.71 us

profile of v2, /device:TPU:1, one launch (start us, length us, event | category | flops | bytes accessed | tf_op | source)
XLA Modules:
  0.0 73.9 jit_solution(2326598399816865686)
XLA Ops:
  0.6 0.0 copy-start
  0.6 0.0 copy-start.1
  0.7 0.0 copy-start.2
  1.4 68.7 %cg_step.1 = (f32[128,1024]{1,0:T(8,128)}, f32[1,1]{1,0:T(1,128)}, f32[1,1]{1,0:T(1,128)}) custom-call(f32[128,1024]{1,0:T(8,128)} %dir_h.1, f32[128,1024]{1,0:T(8,128)} %res_h.1, f32[128,1024]{1,0:T(8,128)} %dec_h.1, bf16[1024,4096]{1,0:T(8,128)(2,1)} %spa_h.1, bf16[1,1,8,128,512]{4,3,2,1,0:T(8,128)(2,1)} %tiles_h.1, s32[1,1,8]{2,1,0:T(1,128)} %tblock_h.1, ...), custom_call_target="tpu_custom_call" | custom-call | flops 2147483648 | bytes 12582912 | tf_op jit(solution)/shard_map/cg_step/pallas_call | solution.py:450
  70.1 0.0 copy-done
  70.1 0.0 copy-done.1
  70.1 0.0 copy-done.2
  70.1 3.7 %multiply_add_fusion = (f32[128,1024]{1,0:T(8,128)}, f32[128,1024]{1,0:T(8,128)}, f32[128,1024]{1,0:T(8,128)}) fusion(f32[128,1024]{1,0:T(8,128)S(1)} %copy-done, f32[]{:T(128)} %bitcast.1, f32[128,1024]{1,0:T(8,128)S(1)} %copy-done.1, f32[128,1024]{1,0:T(8,128)} %get-tuple-element.7, f32[]{:T(128)} %bitcast, f32[128,1024]{1,0:T(8,128)S(1)} %copy-done.2), kind=kLoop, calls=%fused_computation | loop fusion | flops 786432 | bytes 3670024 | tf_op jit(solution)/shard_map/add | solution.py:510
Async XLA Ops:
  0.6 69.5 %copy-start = (f32[128,1024]{1,0:T(8,128)S(1)}, f32[128,1024]{1,0:T(8,128)}, u32[]{:S(2)}) copy-start(f32[128,1024]{1,0:T(8,128)} %dir_h.1) | copy-start | bytes 1572868
  0.6 69.5 %copy-start.1 = (f32[128,1024]{1,0:T(8,128)S(1)}, f32[128,1024]{1,0:T(8,128)}, u32[]{:S(2)}) copy-start(f32[128,1024]{1,0:T(8,128)} %res_h.1) | copy-start | bytes 1572868
  0.7 69.5 %copy-start.2 = (f32[128,1024]{1,0:T(8,128)S(1)}, f32[128,1024]{1,0:T(8,128)}, u32[]{:S(2)}) copy-start(f32[128,1024]{1,0:T(8,128)} %param.11) | copy-start | bytes 1572868

commit v3 on v2

--- a/solution.py
+++ b/solution.py
@@ -17,6 +17,9 @@
 CH = 8
 ST = TW // CH
 PIECES = RC // 128
+KQ = 256
+ORDER = (0, 2, 1, 3)
+CUTS = 4
 DEAD = -8192
 F32 = jnp.float32
 BF16 = jnp.bfloat16
@@ -26,11 +29,11 @@
 
 def kernel(
     dir_h, res_h, dec_h, spa_h, tiles_h, tblock_h, ttime_h, tcell_h, tcount_h, noise_h,
-    img, alpha_o, beta_o,
+    img, ab,
     tblock, ttime, tcell, tcount, noise,
     imgv, dirv, resv, decv, spa, tiles, xa, xb, dp, gp, fp, rp, mx, hx, fstep, bstep, ends,
     abuf, gabuf, bbuf, tbuf, cbuf, ubuf, tabs, chs, ffs, bks, near, obs, red1, red2, sel,
-    lsem, gas, gar, gbs, gbr, as_, ar, a2s, a2r, bs, br, b2s, b2r, cs, cr, c2s, c2r,
+    dsem, lsem, gas, gar, gbs, gbr, as_, ar, a2s, a2r, bs, br, b2s, b2r, cs, cr, c2s, c2r,
     ts, tr, hs, hr, fs, fr, ks, kr, ns, nr, os_, or_, r1s, r1r, r2s, r2r,
 ):
     tm = lax.axis_index("tm")
@@ -38,7 +41,12 @@
     gx = tm // LINE
     gi = lax.rem(tm, LINE)
 
-    loads = [pltpu.make_async_copy(dir_h, dirv, lsem.at[0])]
+    load_dir = {}
+    for q in ORDER:
+        part = slice(KQ * q, KQ * (q + 1))
+        load_dir[q] = pltpu.make_async_copy(dir_h.at[:, part], dirv.at[:, part], dsem.at[q])
+        load_dir[q].start()
+    loads = [pltpu.make_async_copy(noise_h, noise, lsem.at[0])]
     for k in range(REGIONS):
         src = lax.rem(r + REGIONS - k, REGIONS)
         cols = pl.ds(pl.multiple_of(src * RC, RC), RC)
@@ -47,28 +55,29 @@
     loads.append(pltpu.make_async_copy(res_h, resv, lsem.at[6]))
     for n in range(PIECES):
         loads.append(pltpu.make_async_copy(dec_h.at[:, 128 * n : 128 * (n + 1)], decv.at[n], lsem.at[7 + n]))
-    small = ((tcount_h, tcount), (ttime_h, ttime), (tcell_h, tcell), (tblock_h, tblock), (noise_h, noise))
+    small = ((tcount_h, tcount), (ttime_h, ttime), (tcell_h, tcell), (tblock_h, tblock))
     for n, (there, here) in enumerate(small):
         loads.append(pltpu.make_async_copy(there, here, lsem.at[7 + PIECES + n]))
-    load_small = loads[7 + PIECES :]
-    load_dir, load_spa, load_tiles, load_res, load_dec = loads[0], loads[1:5], loads[5], loads[6], loads[7 : 7 + PIECES]
+    load_small = loads[7 + PIECES :] + loads[:1]
+    load_spa, load_tiles, load_res, load_dec = loads[1:5], loads[5], loads[6], loads[7 : 7 + PIECES]
     for c in loads:
         c.start()
 
-    line_peers = [(gx * LINE + lax.rem(gi + k, LINE), r) for k in range(1, LINE)]
+    hops = sorted(range(1, LINE), key=lambda k: -min(k, LINE - k))
+    line_peers = [(gx * LINE + lax.rem(gi + k, LINE), r) for k in hops]
     cross_peers = [(lax.rem(gx + k, LINES) * LINE + gi, r) for k in range(1, LINES)]
     region_peers = [(tm, lax.rem(r + k, REGIONS)) for k in range(1, REGIONS)]
     plane_peers = [
         (lax.rem(gx + kx, LINES) * LINE + gi, lax.rem(r + ky, REGIONS))
-        for kx in range(LINES)
-        for ky in range(REGIONS)
+        for kx in (2, 1, 3, 0)
+        for ky in (2, 1, 3, 0)
         if kx or ky
     ]
     later = [(lax.rem(tm + d, WINDOWS), r) for d in (1, 2)]
     sooner = [(lax.rem(tm + WINDOWS - d, WINDOWS), r) for d in (1, 2)]
 
     barrier = pltpu.get_barrier_semaphore()
-    everyone = line_peers + plane_peers + later + sooner
+    everyone = line_peers + cross_peers + region_peers + later + sooner
     for peer in everyone:
         pl.semaphore_signal(barrier, inc=1, device_id=peer, device_id_type=MESH)
 
@@ -92,43 +101,68 @@
     sub8 = lax.broadcasted_iota(jnp.int32, (CH, RC), 0)
     sub = lax.broadcasted_iota(jnp.int32, (8, 128), 0)
 
-    load_dir.wait()
     row = lax.broadcasted_iota(jnp.int32, (TW, TW), 0)
     col = lax.broadcasted_iota(jnp.int32, (TW, TW), 1)
     moved = jnp.where(lax.rem(row, CH) * ST + row // CH == col, 1.0, 0.0).astype(BF16)
-    xa[0] = jnp.dot(moved, dirv[...].astype(BF16), preferred_element_type=F32).astype(BF16)
-
+
+    def own_part(q):
+        load_dir[q].wait()
+        part = dirv[:, KQ * q : KQ * (q + 1)].astype(BF16)
+        xa[0, q] = jnp.dot(moved, part, preferred_element_type=F32).astype(BF16)
+
+    own_part(ORDER[0])
+    own_part(ORDER[1])
     pl.semaphore_wait(barrier, len(everyone))
 
-    low, high = pl.ds(0, TW // 2), pl.ds(TW // 2, TW // 2)
     right = (tm, lax.rem(r + 1, REGIONS))
     left = (tm, lax.rem(r + REGIONS - 1, REGIONS))
 
-    def gather_start(x, ss, rs):
-        return [
-            send(x.at[0, low], x.at[1, low], ss.at[0], rs.at[0], right),
-            send(x.at[0, high], x.at[3, high], ss.at[1], rs.at[1], left),
-            send(x.at[0, high], x.at[1, high], ss.at[2], rs.at[2], right),
-            send(x.at[0, low], x.at[3, low], ss.at[3], rs.at[3], left),
-        ]
+    def way(q):
+        return (right, 1) if q < 2 else (left, 3)
+
+    def gather_start(x, ss, rs, make):
+        copies = []
+        for n, q in enumerate(ORDER):
+            make(q)
+            peer, slot = way(q)
+            copies.append(send(x.at[0, q], x.at[slot, q], ss.at[n], rs.at[n], peer))
+        for n, (peer, slot, part) in enumerate(((right, 1, pl.ds(2, 2)), (left, 3, pl.ds(0, 2)))):
+            copies.append(send(x.at[0, part], x.at[slot, part], ss.at[4 + n], rs.at[4 + n], peer))
+        return copies
 
     def gather_pass(x, ss, rs, copies):
-        copies[0].wait_recv()
-        copies.append(send(x.at[1, low], x.at[2, low], ss.at[4], rs.at[4], right))
-        copies[1].wait_recv()
-        copies.append(send(x.at[3, high], x.at[2, high], ss.at[5], rs.at[5], left))
-
-    def multiply(x, k, first):
+        for n, q in enumerate(ORDER):
+            peer, slot = way(q)
+            copies[n].wait_recv()
+            copies.append(send(x.at[slot, q], x.at[2, q], ss.at[6 + n], rs.at[6 + n], peer))
+
+    def multiply(x, k, parts, first=False):
         def tile(n, _):
-            cols = pl.ds(pl.multiple_of(n * 256, 256), 256)
-            part = lax.dot_general(x[k], spa[k, cols, :], NT, preferred_element_type=F32)
+            rows = pl.ds(pl.multiple_of(n * 256, 256), 256)
+            total = None
+            for q in parts:
+                part = lax.dot_general(
+                    x[k, q], spa[k, rows, KQ * q : KQ * (q + 1)], NT, preferred_element_type=F32
+                )
+                total = part if total is None else total + part
             if first:
-                mx[:, cols] = part
+                mx[:, rows] = total
             else:
-                mx[:, cols] += part
+                mx[:, rows] += total
             return 0
 
-        lax.fori_loop(0, RC // 256, tile, 0)
+        lax.fori_loop(0, RC // 256, tile, 0, unroll=True)
+
+    def finish(x, copies):
+        multiply(x, 0, ORDER, True)
+        received(copies[4:5])
+        multiply(x, 1, ORDER)
+        received(copies[5:6])
+        multiply(x, 3, ORDER)
+        received(copies[6:8])
+        multiply(x, 2, ORDER[:2])
+        received(copies[8:10])
+        multiply(x, 2, ORDER[2:])
 
     def steps(i):
         return slice(CH * i, CH * (i + 1))
@@ -154,14 +188,14 @@
             buf[2 + d if d else 0] = jnp.where(second_block(d), part[:, FB:], part[:, :FB])
         return [send(buf.at[2 + d], buf.at[d], ss.at[d - 1], rs.at[d - 1], later[d - 1]) for d in (1, 2)]
 
-    copies = gather_start(xa, gas, gar)
+    copies = gather_start(xa, gas, gar, lambda q: own_part(q) if q in ORDER[2:] else None)
 
     for load in load_small:
         load.wait()
+    live = sub < jnp.broadcast_to(tcount[...], (8, 128))
     table = jnp.full((8, 128), DEAD, jnp.int32)
     for s in range(SLOTS):
-        key = jnp.where(s < tcount[0, 0], ttime[0, 0, s] * 2 + tcell[0, 0, s], DEAD)
-        table = jnp.where(sub == s, key, table)
+        table = jnp.where((sub == s) & live, ttime[0, 0, s] * 2 + tcell[0, 0, s], table)
     tabs[0] = table
     table_copies = [
         send(tabs.at[0], tabs.at[d], ts.at[d - 1], tr.at[d - 1], sooner[d - 1]) for d in (1, 2)
@@ -203,7 +237,6 @@
     for load in load_spa:
         load.wait()
 
-    multiply(xa, 0, True)
     received(factor_copies)
     run = jnp.ones((1, RC), F32)
     places = [run] * 3
@@ -229,12 +262,7 @@
         gp[steps(i), :] = jnp.sqrt(1.0 - d * d)
         rp[steps(i), :] = rest
         rest = rest * d
-    received(copies[2:3])
-    multiply(xa, 1, False)
-    received(copies[3:4])
-    multiply(xa, 3, False)
-    received(copies[4:6])
-    multiply(xa, 2, False)
+    finish(xa, copies)
 
     o = jnp.zeros((CH, RC), F32)
     for i in range(ST):
@@ -301,7 +329,7 @@
     back = jnp.zeros((8, FB), F32)
     for s in range(SLOTS):
         row = jnp.sum(jnp.where(sub == tblock[0, 0, s], weighted, 0.0), axis=0, keepdims=True)
-        lhs = jnp.where((sub == s) & (s < tcount[0, 0]), row, 0.0).astype(BF16)
+        lhs = jnp.where((sub == s) & live, row, 0.0).astype(BF16)
         back = back + jnp.dot(lhs, tiles[s], preferred_element_type=F32)
     bks[0] = back
 
@@ -370,22 +398,20 @@
         run = jnp.where(above, gabuf[j - 1, 4] * one + ubuf[j, 2], run)
     far = jnp.where(gi == LINE - 1, two, jnp.where(gi == LINE - 2, one, mine + ends[3, 0:1, :] * run))
     entry = entry + ends[1] * (close + far)
-    for i in range(ST):
-        held = hx[steps(i), :] + rp[steps(i), :] * entry
-        hx[steps(i), :] = gp[steps(i), :] * held
-    xb[0] = lax.dot_general(moved, hx[...].astype(BF16), TN, preferred_element_type=F32).astype(BF16)
-
-    copies = gather_start(xb, gbs, gbr)
-
+
+    def pulled_part(q):
+        part = slice(KQ * q, KQ * (q + 1))
+        for i in range(ST):
+            held = hx[steps(i), part] + rp[steps(i), part] * entry[:, part]
+            hx[steps(i), part] = gp[steps(i), part] * held
+        xb[0, q] = lax.dot_general(
+            moved, hx[:, part].astype(BF16), TN, preferred_element_type=F32
+        ).astype(BF16)
+
+    copies = gather_start(xb, gbs, gbr, pulled_part)
     gather_pass(xb, gbs, gbr, copies)
-    multiply(xb, 0, True)
-    received(copies[2:3])
-    multiply(xb, 1, False)
-    received(copies[3:4])
-    multiply(xb, 3, False)
     load_res.wait()
-    received(copies[4:6])
-    multiply(xb, 2, False)
+    finish(xb, copies)
 
     image = dirv[...] + mx[...]
     imgv[...] = image
@@ -429,11 +455,42 @@
     alpha = norm_old / stats[1:2, :]
     reach = alpha * stats[4:5, :]
     norm_new = jnp.maximum((norm_old - 2.0 * (alpha * stats[2:3, :])) + reach * (reach * stats[3:4, :]), 0.0)
-    alpha_o[...] = alpha[:, 0:1]
-    beta_o[...] = (norm_new / norm_old)[:, 0:1]
+    ab[...] = jnp.where(sub == 0, alpha, norm_new / norm_old)
     store.wait()
     for c in sent:
         c.wait_send()
+
+
+def update(ab_h, img_h, dir_h, res_h, sol_h, sol_o, res_o, dir_o, ab, img, dirv, resv, sol, sn, rn, dn, asem, isem, osem):
+    first = pltpu.make_async_copy(ab_h, ab, asem.at[0])
+    first.start()
+    loads = []
+    for n in range(CUTS):
+        rows = pl.ds(n * (TW // CUTS), TW // CUTS)
+        loads.append(
+            [
+                pltpu.make_async_copy(far.at[rows], near.at[rows], isem.at[n, k])
+                for k, (far, near) in enumerate(((img_h, img), (dir_h, dirv), (res_h, resv), (sol_h, sol)))
+            ]
+        )
+        for load in loads[n]:
+            load.start()
+    first.wait()
+    alpha, beta = ab[0:1, 0:1], ab[1:2, 0:1]
+    stores = []
+    for n in range(CUTS):
+        rows = pl.ds(n * (TW // CUTS), TW // CUTS)
+        for load in loads[n]:
+            load.wait()
+        left = resv[rows, :] - alpha * img[rows, :]
+        rn[rows, :] = left
+        sn[rows, :] = sol[rows, :] + alpha * dirv[rows, :]
+        dn[rows, :] = left + beta * dirv[rows, :]
+        for k, (near, far) in enumerate(((sn, sol_o), (rn, res_o), (dn, dir_o))):
+            stores.append(pltpu.make_async_copy(near.at[rows], far.at[rows], osem.at[n, k]))
+            stores[-1].start()
+    for store in stores:
+        store.wait()
 
 
 def body(
@@ -444,23 +501,22 @@
     vmem = pl.BlockSpec(memory_space=pltpu.VMEM)
     vector = (1, RC)
     dma = pltpu.SemaphoreType.DMA
-    sems = [13 + PIECES, 6, 6, 6, 6]
+    sems = [4, 13 + PIECES, 10, 10, 10, 10]
     for n in (LINE - 1, LINES - 1) * 3 + (2, 2, 2, 2, 2, REGIONS - 1, LINE - 1, LINES * REGIONS - 1):
         sems += [n, n]
-    image, alpha, beta = pl.pallas_call(
+    image, ab = pl.pallas_call(
         kernel,
         out_shape=(
             jax.ShapeDtypeStruct((TW, RC), F32),
-            jax.ShapeDtypeStruct((1, 1), F32),
-            jax.ShapeDtypeStruct((1, 1), F32),
+            jax.ShapeDtypeStruct((8, 128), F32),
         ),
         in_specs=[hbm] * 10,
-        out_specs=(hbm, vmem, vmem),
+        out_specs=(hbm, vmem),
         scratch_shapes=[
             pltpu.SMEM((1, 1, SLOTS), jnp.int32),
             pltpu.SMEM((1, 1, SLOTS), jnp.int32),
             pltpu.SMEM((1, 1, SLOTS), jnp.int32),
-            pltpu.SMEM((1, 1), jnp.int32),
+            pltpu.VMEM((1, 1), jnp.int32),
             pltpu.VMEM((8, 128), F32),
             pltpu.VMEM((TW, RC), F32),
             pltpu.VMEM((TW, RC), F32),
@@ -468,8 +524,8 @@
             pltpu.VMEM((PIECES, TW, 128), F32),
             pltpu.VMEM((REGIONS, RC, RC), BF16),
             pltpu.VMEM((SLOTS, 128, FB), BF16),
-            pltpu.VMEM((REGIONS, TW, RC), BF16),
-            pltpu.VMEM((REGIONS, TW, RC), BF16),
+            pltpu.VMEM((REGIONS, RC // KQ, TW, KQ), BF16),
+            pltpu.VMEM((REGIONS, RC // KQ, TW, KQ), BF16),
             pltpu.VMEM((TW, RC), F32),
             pltpu.VMEM((TW, RC), F32),
             pltpu.VMEM((TW, RC), F32),
@@ -504,10 +560,18 @@
         ),
         name="cg_step",
     )(direction, residual, decay, spatial, tiles, tile_block, tile_time, tile_cell, tile_count, noise_inv)
-    alpha = alpha[0, 0]
-    beta = beta[0, 0]
-    residual_new = residual - alpha * image
-    return (solution + alpha * direction, residual_new, residual_new + beta * direction)
+    block = jax.ShapeDtypeStruct((TW, RC), F32)
+    return pl.pallas_call(
+        update,
+        out_shape=(block,) * 3,
+        in_specs=[hbm] * 5,
+        out_specs=(hbm,) * 3,
+        scratch_shapes=[pltpu.VMEM((8, 128), F32)]
+        + [pltpu.VMEM((TW, RC), F32)] * 7
+        + [dma((1,)), dma((CUTS, 4)), dma((CUTS, 3))],
+        cost_estimate=pl.CostEstimate(flops=6 * TW * RC, bytes_accessed=28 * TW * RC, transcendentals=0),
+        name="cg_update",
+    )(ab, image, direction, residual, solution)
 
 
 def solution(mesh):

time: 74 us -> 71.3 us (0.964)
  other arithmetic: 3.71 us -> 0 us
  Pallas kernels: 68.7 us -> 69.9 us
    add x1 -> x0, other arithmetic: 3.71 us -> none  [body(): residual_new + beta * direction]
    pallas_call x0 -> x1, Pallas kernels: none -> 2.79 us  [body(): pl.pallas_call(update, out_shape=(block,) * 3, in_specs=[hbm] * 5, out_sp...]
    pallas_call x1, Pallas kernels: 68.7 us -> 67.1 us  [body(): pl.pallas_call(kernel, out_shape=(jax.ShapeDtypeStruct((TW, RC), F32), ja...]
where the time goes in v3:
time: 71.3 us; the launch traced here: 71.2 us
  Pallas kernels  69.9 us (98%)
  between operations  1.29 us (2%)
    pallas_call x1, Pallas kernels, body(): pl.pallas_call(kernel, out_shape=(jax.ShapeDtypeStruct((TW, RC), F32), ja...  67.1 us
    pallas_call x1, Pallas kernels, body(): pl.pallas_call(update, out_shape=(block,) * 3, in_specs=[hbm] * 5, out_sp...  2.79 us

profile of v3, /device:TPU:1, one launch (start us, length us, event | category | flops | bytes accessed | tf_op | source)
XLA Modules:
  0.0 71.2 jit_solution(7444720507503923485)
XLA Ops:
  1.3 67.1 %cg_step.1 = (f32[128,1024]{1,0:T(8,128)}, f32[8,128]{1,0:T(8,128)}) custom-call(f32[128,1024]{1,0:T(8,128)} %dir_h.3, f32[128,1024]{1,0:T(8,128)} %res_h.3, f32[128,1024]{1,0:T(8,128)} %dec_h.1, bf16[1024,4096]{1,0:T(8,128)(2,1)} %spa_h.1, bf16[1,1,8,128,512]{4,3,2,1,0:T(8,128)(2,1)} %tiles_h.1, s32[1,1,8]{2,1,0:T(1,128)} %tblock_h.1, s32[1,1,8]{2,1,0:T(1,128)} %ttime_h.1, ...), custom_call_target="tpu_custom_call" | custom-call | flops 2147483648 | bytes 12582912 | tf_op jit(solution)/shard_map/cg_step/pallas_call | solution.py:507
  68.4 2.8 %cg_update.1 = (f32[128,1024]{1,0:T(8,128)}, f32[128,1024]{1,0:T(8,128)}, f32[128,1024]{1,0:T(8,128)}) custom-call(f32[8,128]{1,0:T(8,128)} %get-tuple-element.5.ab_h, f32[128,1024]{1,0:T(8,128)} %get-tuple-element.6.img_h, f32[128,1024]{1,0:T(8,128)} %dir_h.3, f32[128,1024]{1,0:T(8,128)} %res_h.3, f32[128,1024]{1,0:T(8,128)} %sol_h.1), custom_call_target="tpu_custom_call" | custom-call | flops 786432 | bytes 3670016 | tf_op jit(solution)/shard_map/cg_update/pallas_call | solution.py:564

commit v4 on v3

--- a/solution.py
+++ b/solution.py
@@ -19,7 +19,7 @@
 PIECES = RC // 128
 KQ = 256
 ORDER = (0, 2, 1, 3)
-CUTS = 4
+CUTS = 2
 DEAD = -8192
 F32 = jnp.float32
 BF16 = jnp.bfloat16
@@ -172,6 +172,9 @@
         left_over = x - first.astype(F32)
         second = left_over.astype(BF16)
         return first, second, (left_over - second.astype(F32)).astype(BF16)
+
+    def whole(x):
+        return jnp.sum(jnp.sum(x, axis=0, keepdims=True), axis=1, keepdims=True)
 
     def second_block(d):
         cell = lax.bitwise_and(tabs[d], 1) == 1
@@ -223,6 +226,8 @@
         b = b * jnp.where(sub8 < CH - k, pltpu.roll(b, CH - k, 0), 1.0)
     ends[1] = jnp.where(sub8 < CH - 1, pltpu.roll(b, CH - 1, 0), 1.0)
 
+    gather_pass(xa, gas, gar, copies)
+
     received(table_copies)
     time_of = lax.broadcasted_iota(jnp.int32, (8, 128), 1)
     time_of = lax.rem(time_of, CH) * ST + time_of // CH
@@ -233,7 +238,6 @@
         sel[8 * d : 8 * d + 8, :] = jnp.where(local == time_of, 1.0, 0.0)
     sel[24:32, :] = jnp.zeros((8, 128), F32)
     factor_rows = hand_on(hx[...], ffs, fs, fr)
-    gather_pass(xa, gas, gar, copies)
     for load in load_spa:
         load.wait()
 
@@ -411,6 +415,8 @@
     copies = gather_start(xb, gbs, gbr, pulled_part)
     gather_pass(xb, gbs, gbr, copies)
     load_res.wait()
+    res = resv[...]
+    norm_here = whole(res * res)
     finish(xb, copies)
 
     image = dirv[...] + mx[...]
@@ -418,9 +424,6 @@
     store = pltpu.make_async_copy(imgv, img, lsem.at[12 + PIECES])
     store.start()
 
-    def whole(x):
-        return jnp.sum(jnp.sum(x, axis=0, keepdims=True), axis=1, keepdims=True)
-
     def inverse(x):
         ok = x > 1e-37
         return jnp.where(ok, 1.0 / jnp.where(ok, x, 1.0), 0.0)
@@ -428,7 +431,7 @@
     res = resv[...]
     largest = jnp.max(jnp.max(jnp.abs(image), axis=0, keepdims=True), axis=1, keepdims=True)
     scaled = image * inverse(largest)
-    stats = jnp.where(sub == 0, whole(res * res), 0.0)
+    stats = jnp.where(sub == 0, norm_here, 0.0)
     stats = jnp.where(sub == 1, whole(dirv[...] * image), stats)
     stats = jnp.where(sub == 2, whole(res * image), stats)
     stats = jnp.where(sub == 3, whole(scaled * scaled), stats)
@@ -446,8 +449,13 @@
         return jnp.where(sub == 4, top, out)
 
     red1[gi] = stats
-    received(to_all(red1.at[gi], r1s, r1r, line_peers))
+    older = list(sent)
+    copies = to_all(red1.at[gi], r1s, r1r, line_peers)
+    for c in older:
+        c.wait_send()
+    received(copies)
     here = gx * REGIONS + r
+    store.wait()
     red2[here] = merged(red1, LINE)
     received(to_all(red2.at[here], r2s, r2r, plane_peers))
     stats = merged(red2, LINES * REGIONS)
@@ -456,8 +464,7 @@
     reach = alpha * stats[4:5, :]
     norm_new = jnp.maximum((norm_old - 2.0 * (alpha * stats[2:3, :])) + reach * (reach * stats[3:4, :]), 0.0)
     ab[...] = jnp.where(sub == 0, alpha, norm_new / norm_old)
-    store.wait()
-    for c in sent:
+    for c in sent[len(older) :]:
         c.wait_send()
 
 

time: 71.3 us -> 71.1 us (level)
  no operation moved by 1% of the time
where the time goes in v4:
time: 71.1 us; the launch traced here: 70.9 us
  Pallas kernels  69.7 us (98%)
  between operations  1.29 us (2%)
    pallas_call x1, Pallas kernels, body(): pl.pallas_call(kernel, out_shape=(jax.ShapeDtypeStruct((TW, RC), F32), ja...  67 us
    pallas_call x1, Pallas kernels, body(): pl.pallas_call(update, out_shape=(block,) * 3, in_specs=[hbm] * 5, out_sp...  2.65 us

profile of v4, /device:TPU:1, one launch (start us, length us, event | category | flops | bytes accessed | tf_op | source)
XLA Modules:
  0.0 70.9 jit_solution(10286381291035229772)
XLA Ops:
  1.3 67.0 %cg_step.1 = (f32[128,1024]{1,0:T(8,128)}, f32[8,128]{1,0:T(8,128)}) custom-call(f32[128,1024]{1,0:T(8,128)} %dir_h.3, f32[128,1024]{1,0:T(8,128)} %res_h.3, f32[128,1024]{1,0:T(8,128)} %dec_h.1, bf16[1024,4096]{1,0:T(8,128)(2,1)} %spa_h.1, bf16[1,1,8,128,512]{4,3,2,1,0:T(8,128)(2,1)} %tiles_h.1, s32[1,1,8]{2,1,0:T(1,128)} %tblock_h.1, s32[1,1,8]{2,1,0:T(1,128)} %ttime_h.1, ...), custom_call_target="tpu_custom_call" | custom-call | flops 2147483648 | bytes 12582912 | tf_op jit(solution)/shard_map/cg_step/pallas_call | solution.py:514
  68.3 2.7 %cg_update.1 = (f32[128,1024]{1,0:T(8,128)}, f32[128,1024]{1,0:T(8,128)}, f32[128,1024]{1,0:T(8,128)}) custom-call(f32[8,128]{1,0:T(8,128)} %get-tuple-element.5.ab_h, f32[128,1024]{1,0:T(8,128)} %get-tuple-element.6.img_h, f32[128,1024]{1,0:T(8,128)} %dir_h.3, f32[128,1024]{1,0:T(8,128)} %res_h.3, f32[128,1024]{1,0:T(8,128)} %sol_h.1), custom_call_target="tpu_custom_call" | custom-call | flops 786432 | bytes 3670016 | tf_op jit(solution)/shard_map/cg_update/pallas_call | solution.py:571

commit v5 on v4

--- a/solution.py
+++ b/solution.py
@@ -153,12 +153,12 @@
 
         lax.fori_loop(0, RC // 256, tile, 0, unroll=True)
 
-    def finish(x, copies):
-        multiply(x, 0, ORDER, True)
+    def finish(x, copies, between=lambda: None):
         received(copies[4:5])
         multiply(x, 1, ORDER)
         received(copies[5:6])
         multiply(x, 3, ORDER)
+        between()
         received(copies[6:8])
         multiply(x, 2, ORDER[:2])
         received(copies[8:10])
@@ -217,16 +217,49 @@
         f = f * jnp.where(sub8 >= k, pltpu.roll(f, k, 0), 1.0)
     abuf[gi] = f[CH - 1 : CH, :]
     factor_copies = to_all(abuf.at[gi], as_, ar, line_peers)
-    chunk_before = jnp.where(sub8 >= 1, pltpu.roll(f, 1, 0), 1.0)
     for i in range(ST):
-        hx[steps(i), :] = fp[steps(i), :] * chunk_before
-    b = total
+        d = dp[steps(i), :]
+        gp[steps(i), :] = jnp.sqrt(1.0 - d * d)
+    ends[0] = jnp.where(sub8 >= 1, pltpu.roll(f, 1, 0), 1.0)
+    ends[1] = total
+    for load in load_spa:
+        load.wait()
+    multiply(xa, 0, ORDER, True)
+    gather_pass(xa, gas, gar, copies)
+
+    cross = []
+
+    def line_factors():
+        received(factor_copies)
+        run = jnp.ones((1, RC), F32)
+        places = [run] * 3
+        for j in range(LINE):
+            for n in range(3):
+                places[n] = jnp.where(j == gi - n, run, places[n])
+            if j >= LINE - 2:
+                gabuf[gx, LINE - j] = run
+            run = run * abuf[j]
+        gabuf[gx, 0] = run
+        gabuf[gx, 3] = abuf[LINE - 1]
+        gabuf[gx, 4] = abuf[LINE - 2]
+        cross.extend(to_all(gabuf.at[gx], a2s, a2r, cross_peers))
+        for n in range(3):
+            ends[2, n : n + 1, :] = places[n]
+        run = jnp.ones((1, RC), F32)
+        for j in range(3, LINE):
+            run = run * jnp.where(j >= gi + 3, abuf[j - 2], 1.0)
+        ends[3, 0:1, :] = run
+
+    finish(xa, copies, line_factors)
+
+    o = jnp.zeros((CH, RC), F32)
+    for i in range(ST):
+        o = dp[steps(i), :] * o + gp[steps(i), :] * mx[steps(i), :]
+        mx[steps(i), :] = o
     for n, k in enumerate((1, 2, 4)):
-        bstep[n] = b
-        b = b * jnp.where(sub8 < CH - k, pltpu.roll(b, CH - k, 0), 1.0)
-    ends[1] = jnp.where(sub8 < CH - 1, pltpu.roll(b, CH - 1, 0), 1.0)
-
-    gather_pass(xa, gas, gar, copies)
+        o = o + fstep[n] * jnp.where(sub8 >= k, pltpu.roll(o, k, 0), 0.0)
+    bbuf[gi] = o[CH - 1 : CH, :]
+    line_copies = to_all(bbuf.at[gi], bs, br, line_peers)
 
     received(table_copies)
     time_of = lax.broadcasted_iota(jnp.int32, (8, 128), 1)
@@ -237,52 +270,15 @@
         local = lax.shift_right_arithmetic(tabs[d], 1) + (d - 2) * TW
         sel[8 * d : 8 * d + 8, :] = jnp.where(local == time_of, 1.0, 0.0)
     sel[24:32, :] = jnp.zeros((8, 128), F32)
-    factor_rows = hand_on(hx[...], ffs, fs, fr)
-    for load in load_spa:
-        load.wait()
-
-    received(factor_copies)
-    run = jnp.ones((1, RC), F32)
-    places = [run] * 3
-    for j in range(LINE):
-        for n in range(3):
-            places[n] = jnp.where(j == gi - n, run, places[n])
-        if j >= LINE - 2:
-            gabuf[gx, LINE - j] = run
-        run = run * abuf[j]
-    gabuf[gx, 0] = run
-    gabuf[gx, 3] = abuf[LINE - 1]
-    gabuf[gx, 4] = abuf[LINE - 2]
-    cross_copies = to_all(gabuf.at[gx], a2s, a2r, cross_peers)
-    for n in range(3):
-        ends[2, n : n + 1, :] = places[n]
-    run = jnp.ones((1, RC), F32)
-    for j in range(3, LINE):
-        run = run * jnp.where(j >= gi + 3, abuf[j - 2], 1.0)
-    ends[3, 0:1, :] = run
-    rest = jnp.ones((CH, RC), F32)
-    for i in reversed(range(ST)):
-        d = dp[steps(i), :]
-        gp[steps(i), :] = jnp.sqrt(1.0 - d * d)
-        rp[steps(i), :] = rest
-        rest = rest * d
-    finish(xa, copies)
-
-    o = jnp.zeros((CH, RC), F32)
-    for i in range(ST):
-        o = dp[steps(i), :] * o + gp[steps(i), :] * mx[steps(i), :]
-        mx[steps(i), :] = o
-    for n, k in enumerate((1, 2, 4)):
-        o = o + fstep[n] * jnp.where(sub8 >= k, pltpu.roll(o, k, 0), 0.0)
-    bbuf[gi] = o[CH - 1 : CH, :]
-    line_copies = to_all(bbuf.at[gi], bs, br, line_peers)
 
     entry = jnp.where(sub8 >= 1, pltpu.roll(o, 1, 0), 0.0)
     for i in range(ST):
         mx[steps(i), :] = mx[steps(i), :] + fp[steps(i), :] * entry
     row_copies = hand_on(mx[...], chs, hs, hr)
-    received(cross_copies)
-    received(factor_rows)
+    for i in range(ST):
+        hx[steps(i), :] = fp[steps(i), :] * ends[0]
+    factor_rows = hand_on(hx[...], ffs, fs, fr)
+    received(cross)
     before = lax.rem(gx + LINES - 1, LINES)
     ends[3, 1:2, :] = jnp.where(gi >= 1, abuf[lax.rem(gi + LINE - 1, LINE)], gabuf[before, 3])
     ends[3, 2:3, :] = jnp.where(
@@ -299,6 +295,16 @@
         run = abuf[j] * run + bbuf[j]
     tbuf[gx, 0] = run
     cross_copies = to_all(tbuf.at[gx], b2s, b2r, cross_peers)
+    b = ends[1]
+    for n, k in enumerate((1, 2, 4)):
+        bstep[n] = b
+        b = b * jnp.where(sub8 < CH - k, pltpu.roll(b, CH - k, 0), 1.0)
+    ends[1] = jnp.where(sub8 < CH - 1, pltpu.roll(b, CH - 1, 0), 1.0)
+    rest = jnp.ones((CH, RC), F32)
+    for i in reversed(range(ST)):
+        rp[steps(i), :] = rest
+        rest = rest * dp[steps(i), :]
+    received(factor_rows)
     received(row_copies)
     received(cross_copies)
     run = jnp.zeros((1, RC), F32)
@@ -413,6 +419,7 @@
         ).astype(BF16)
 
     copies = gather_start(xb, gbs, gbr, pulled_part)
+    multiply(xb, 0, ORDER, True)
     gather_pass(xb, gbs, gbr, copies)
     load_res.wait()
     res = resv[...]

time: 71.1 us -> 71.1 us (level)
  no operation moved by 1% of the time
where the time goes in v5:
time: 71.1 us; the launch traced here: 71 us
  Pallas kernels  69.7 us (98%)
  between operations  1.29 us (2%)
    pallas_call x1, Pallas kernels, body(): pl.pallas_call(kernel, out_shape=(jax.ShapeDtypeStruct((TW, RC), F32), ja...  67 us
    pallas_call x1, Pallas kernels, body(): pl.pallas_call(update, out_shape=(block,) * 3, in_specs=[hbm] * 5, out_sp...  2.65 us

profile of v5, /device:TPU:1, one launch (start us, length us, event | category | flops | bytes accessed | tf_op | source)
XLA Modules:
  0.0 71.0 jit_solution(7845249669471133053)
XLA Ops:
  1.3 67.0 %cg_step.1 = (f32[128,1024]{1,0:T(8,128)}, f32[8,128]{1,0:T(8,128)}) custom-call(f32[128,1024]{1,0:T(8,128)} %dir_h.3, f32[128,1024]{1,0:T(8,128)} %res_h.3, f32[128,1024]{1,0:T(8,128)} %dec_h.1, bf16[1024,4096]{1,0:T(8,128)(2,1)} %spa_h.1, bf16[1,1,8,128,512]{4,3,2,1,0:T(8,128)(2,1)} %tiles_h.1, s32[1,1,8]{2,1,0:T(1,128)} %tblock_h.1, s32[1,1,8]{2,1,0:T(1,128)} %ttime_h.1, ...), custom_call_target="tpu_custom_call" | custom-call | flops 2147483648 | bytes 12582912 | tf_op jit(solution)/shard_map/cg_step/pallas_call | solution.py:521
  68.3 2.7 %cg_update.1 = (f32[128,1024]{1,0:T(8,128)}, f32[128,1024]{1,0:T(8,128)}, f32[128,1024]{1,0:T(8,128)}) custom-call(f32[8,128]{1,0:T(8,128)} %get-tuple-element.5.ab_h, f32[128,1024]{1,0:T(8,128)} %get-tuple-element.6.img_h, f32[128,1024]{1,0:T(8,128)} %dir_h.3, f32[128,1024]{1,0:T(8,128)} %res_h.3, f32[128,1024]{1,0:T(8,128)} %sol_h.1), custom_call_target="tpu_custom_call" | custom-call | flops 786432 | bytes 3670016 | tf_op jit(solution)/shard_map/cg_update/pallas_call | solution.py:578
